TPU v7x, 32 devices: a whole 2x2x4 slice. The times are simulated.
32 devices in a mesh: grp: 4 (over y, x), sp: 8 (over z, core).
Axes of the slice: x: 2, y: 2, z: 4, core: 2. Of those that a mesh axis runs over, the one named last changes fastest.
Arguments:
- queries: bfloat16 [4, 512, 1024], P('grp', 'sp'), may hold values from -180 to 180
- keys: bfloat16 [4, 512, 1024], P('grp', 'sp'), may hold values from -7 to 7
- values: bfloat16 [4, 512, 1024], P('grp', 'sp'), may hold values from -6 to 6
- positions: int32 [4, 512], P('grp'), may hold values from 0 to 511, each once within a row
- anchor: int32 [1], replicated, may hold values from 0 to 262143
Outputs:
- attended: bfloat16 [4, 512, 1024], P('grp', 'sp')
Inputs may be any that keep to these rules, and one draw needn't show every extreme that they name: Each group's row of positions holds every number of 0 to 511 once.
All inputs are finite; a program needn't handle non-finite values.
Results may differ from a plain program's by a relative error of at most 0.0048.
Values may be sent and summed in bfloat16 or wider, within the bound.
No kernel may reach another device: no remote copies, remote signals or barrier semaphores. Data moves between devices by JAX's collectives and lax.ppermute only.
A program may use at most 64 MiB of HBM per device.

v0:
```python
import math

import jax
import jax.numpy as jnp
from jax import lax
from jax.sharding import PartitionSpec as P

HD = 128


NEG = -1e30


def broadcast(block, axis, source):
    block = jnp.where(lax.axis_index(axis) == source, block, jnp.zeros_like(block))
    return lax.psum(block, axis)


def attend(q_heads, k_heads, v_heads, ak_heads, av_heads, order, skip_anchor):
    length, width = q_heads.shape
    head_count = width // HD
    block_rows = min(512, length)
    block_count = length // block_rows
    score_scale = 1.0 / math.sqrt(HD)
    key_rows = jnp.concatenate([k_heads, ak_heads], 0).reshape(2 * length, head_count, HD)
    value_rows = jnp.concatenate([v_heads, av_heads], 0).reshape(2 * length, head_count, HD)
    query_blocks = q_heads.reshape(block_count, block_rows, head_count, HD)
    order_blocks = order.reshape(block_count, block_rows)

    def one_block(pieces):
        query_block, query_order = pieces
        scores = (
            jnp.einsum("qhd,khd->hqk", query_block, key_rows, preferred_element_type=jnp.float32)
            * score_scale
        )
        visible = order[None, :] <= query_order[:, None]
        local_part = jnp.where(visible[None], scores[:, :, :length], NEG)
        far_part = jnp.where(skip_anchor, NEG, scores[:, :, length:])
        joined = jnp.concatenate([local_part, far_part], 2)
        top_score = jnp.max(joined, axis=2, keepdims=True)
        expo = jnp.exp(joined - top_score)
        probs = (expo / jnp.sum(expo, axis=2, keepdims=True)).astype(jnp.bfloat16)
        output = jnp.einsum("hqk,khd->qhd", probs, value_rows, preferred_element_type=jnp.float32)
        return output.astype(jnp.bfloat16).reshape(block_rows, width)

    return lax.map(one_block, (query_blocks, order_blocks)).reshape(length, width)


def on_device(queries, keys, values, positions, anchor):
    group_count = lax.axis_size("grp")
    anchor_root = anchor[0] % group_count
    group_index = lax.axis_index("grp")
    q_heads, k_heads, v_heads = (
        lax.all_to_all(queries, "sp", split_axis=2, concat_axis=1, tiled=True),
        lax.all_to_all(keys, "sp", split_axis=2, concat_axis=1, tiled=True),
        lax.all_to_all(values, "sp", split_axis=2, concat_axis=1, tiled=True),
    )
    ak_heads, av_heads = (
        broadcast(k_heads, "grp", anchor_root),
        broadcast(v_heads, "grp", anchor_root),
    )
    attended_heads = attend(
        q_heads[0],
        k_heads[0],
        v_heads[0],
        ak_heads[0],
        av_heads[0],
        positions[0],
        group_index == anchor_root,
    )
    restored = lax.all_to_all(attended_heads[None], "sp", split_axis=1, concat_axis=2, tiled=True)
    return restored


def solution(mesh):
    return jax.shard_map(
        on_device,
        mesh=mesh,
        in_specs=(
            P("grp", "sp", None),
            P("grp", "sp", None),
            P("grp", "sp", None),
            P("grp", None),
            P(),
        ),
        out_specs=P("grp", "sp", None),
        check_vma=False,
    )
```

profile of v0, /device:TPU:0, one launch (start us, length us, event | category | flops | bytes accessed | tf_op | source)
XLA Modules:
  0.0 112.8 jit_solution(6423109438899094443)
XLA Ops:
  6.5 0.0 copy-start
  6.5 0.0 copy-start.1
  6.5 1.2 %copy.23 = bf16[1,64,1024]{1,0,2:T(2,128)(2,1)S(1)} copy(bf16[1,64,1024]{2,1,0:T(8,128)(2,1)} %param.5) | data formatting | bytes 262144 | tf_op args[0]
  7.8 0.6 broadcast.126
  8.4 2.2 %reduce.5 = bf16[1024,64]{1,0:T(8,128)(2,1)S(1)} reduce(bf16[1024,1,64]{2,1,0:T(2,128)(2,1)S(1)} %bitcast.76, bf16[]{:T(256)} %broadcast.126), dimensions={1}, to_apply=%bitcast.54.reduce_sub_computation | reduce | bytes 262146
  10.6 0.9 reshape.230
  11.5 6.3 %all-to-all-start.2 = ((bf16[8,2,4096]{2,1,0:T(2,128)(2,1)}), bf16[8,2,4096]{2,1,0:T(2,128)(2,1)S(1)}, u32[]{:S(2)}, u32[]{:S(2)}) async-start(bf16[8,2,4096]{2,1,0:T(2,128)(2,1)} %reshape.230), calls=%async_computation.2 | async-start | bytes 262144 | tf_op jit(solution)/shard_map/all_to_all | solution.py:54
  17.8 0.0 copy-done
  17.8 0.4 copy.19
  18.2 2.3 %reduce.6 = bf16[1024,64]{1,0:T(8,128)(2,1)S(1)} reduce(bf16[1024,1,64]{2,1,0:T(2,128)(2,1)S(1)} %bitcast.77, bf16[]{:T(256)} %broadcast.126), dimensions={1}, to_apply=%bitcast.56.reduce_sub_computation | reduce | bytes 262146
  20.5 0.9 reshape.232
  21.4 3.2 %all-to-all-done.2 = bf16[8,2,4096]{2,1,0:T(2,128)(2,1)S(1)} async-done(((bf16[8,2,4096]{2,1,0:T(2,128)(2,1)}), bf16[8,2,4096]{2,1,0:T(2,128)(2,1)S(1)}, u32[]{:S(2)}, u32[]{:S(2)}) %all-to-all-start.2) | async-done | bytes 131104 | tf_op jit(solution)/shard_map/all_to_all | solution.py:54
  24.6 3.4 %all-to-all-start.1 = ((bf16[8,2,4096]{2,1,0:T(2,128)(2,1)}), bf16[8,2,4096]{2,1,0:T(2,128)(2,1)S(1)}, u32[]{:S(2)}, u32[]{:S(2)}) async-start(bf16[8,2,4096]{2,1,0:T(2,128)(2,1)} %reshape.232), calls=%async_computation.1 | async-start | bytes 262144 | tf_op jit(solution)/shard_map/all_to_all | solution.py:55
  28.7 0.0 copy-done.1
  28.7 0.4 copy.15
  29.1 2.3 %reduce.7 = bf16[1024,64]{1,0:T(8,128)(2,1)S(1)} reduce(bf16[1024,1,64]{2,1,0:T(2,128)(2,1)S(1)} %bitcast.78, bf16[]{:T(256)} %broadcast.126), dimensions={1}, to_apply=%bitcast.58.reduce_sub_computation | reduce | bytes 262146
  31.3 0.9 reshape.234
  32.2 0.3 reshape.231
  32.5 0.3 copy.24
  32.9 1.8 %all-to-all-done.1 = bf16[8,2,4096]{2,1,0:T(2,128)(2,1)S(1)} async-done(((bf16[8,2,4096]{2,1,0:T(2,128)(2,1)}), bf16[8,2,4096]{2,1,0:T(2,128)(2,1)S(1)}, u32[]{:S(2)}, u32[]{:S(2)}) %all-to-all-start.1) | async-done | bytes 131104 | tf_op jit(solution)/shard_map/all_to_all | solution.py:55
  34.7 3.4 %all-to-all-start = ((bf16[8,2,4096]{2,1,0:T(2,128)(2,1)}), bf16[8,2,4096]{2,1,0:T(2,128)(2,1)S(1)}, u32[]{:S(2)}, u32[]{:S(2)}) async-start(bf16[8,2,4096]{2,1,0:T(2,128)(2,1)} %reshape.234), calls=%async_computation | async-start | bytes 262144 | tf_op jit(solution)/shard_map/all_to_all | solution.py:56
  38.1 0.0 all-reduce.3.cloned.1.call-start
  38.1 0.3 reshape.233
  38.5 0.3 copy.20
  38.9 6.0 %all-to-all-done = bf16[8,2,4096]{2,1,0:T(2,128)(2,1)S(1)} async-done(((bf16[8,2,4096]{2,1,0:T(2,128)(2,1)}), bf16[8,2,4096]{2,1,0:T(2,128)(2,1)S(1)}, u32[]{:S(2)}, u32[]{:S(2)}) %all-to-all-start) | async-done | bytes 131104 | tf_op jit(solution)/shard_map/all_to_all | solution.py:56
  44.8 0.3 reshape.235
  45.1 0.3 copy.16
  45.5 0.7 copy.22
  46.2 0.7 copy.18
  46.9 0.0 copy-start.2
  46.9 0.0 all-reduce.3.cloned.1.call-update
  47.0 42.1 %all-reduce.3.cloned.1.call-done = (bf16[512,128]{1,0:T(8,128)(2,1)}, bf16[512,128]{1,0:T(8,128)(2,1)}) async-done(((bf16[512,128]{1,0:T(8,128)(2,1)}, bf16[512,128]{1,0:T(8,128)(2,1)}), (bf16[512,128]{1,0:T(8,128)(2,1)}, bf16[512,128]{1,0:T(8,128)(2,1)})) %all-reduce.3.cloned.1.call-update) | async-done | bytes 262160 | tf_op jit(solution)/shard_map/psum | solution.py:16
  89.2 1.3 %multiply_bitcast_fusion = f32[1,512,1024]{1,2,0:T(8,128)S(1)} fusion(bf16[512,128]{1,0:T(8,128)(2,1)S(1)} %bitcast.85, bf16[512,128]{1,0:T(8,128)(2,1)} %get-tuple-element.17, bf16[512,128]{1,0:T(8,128)(2,1)S(1)} %bitcast.86), kind=kOutput, calls=%fused_computation.6 | convolution fusion | flops 135266304 | bytes 2490368 | tf_op jit(solution)/shard_map/while/body/eval_jaxpr/qhd,khd->hqk/dot_general | solution.py:33
  90.5 0.0 copy-done.2
  90.5 0.4 fusion.17
  90.9 0.0 copy-start.3
  90.9 0.4 fusion.3
  91.3 0.5 copy-done.3
  91.8 0.5 fusion.5
  92.3 0.2 copy.26
  92.5 1.4 %reduce.8 = bf16[512,128]{1,0:T(8,128)(2,1)S(1)} reduce(bf16[512,1,128]{2,1,0:T(2,128)(2,1)S(1)} %bitcast.83, bf16[]{:T(256)} %broadcast.126), dimensions={1}, to_apply=%bitcast.60.reduce_sub_computation | reduce | bytes 262146
  93.9 11.2 %all_to_all.63 = bf16[8,2,4096]{2,1,0:T(2,128)(2,1)S(1)} all-to-all(bf16[8,2,4096]{2,1,0:T(2,128)(2,1)S(1)} %reshape.236), channel_id=1, replica_groups=mesh['grp'=4,'sp'=8] {'sp'}, dimensions={0} | all-to-all | bytes 262144 | tf_op jit(solution)/shard_map/all_to_all | solution.py:71
  105.1 0.1 reshape.237
  105.3 0.7 copy.34
  (13 shorter events, 0.2 us)
Async XLA Ops:
  6.5 11.3 %copy-start = (bf16[1,64,1024]{2,1,0:T(8,128)(2,1)S(1)}, bf16[1,64,1024]{2,1,0:T(8,128)(2,1)}, u32[]{:S(2)}) copy-start(bf16[1,64,1024]{2,1,0:T(8,128)(2,1)} %param.6) | copy-start | bytes 393220
  6.5 22.1 %copy-start.1 = (bf16[1,64,1024]{2,1,0:T(8,128)(2,1)S(1)}, bf16[1,64,1024]{2,1,0:T(8,128)(2,1)}, u32[]{:S(2)}) copy-start(bf16[1,64,1024]{2,1,0:T(8,128)(2,1)} %param.7) | copy-start | bytes 393220
  11.5 13.1 %all-to-all-start.2 = ((bf16[8,2,4096]{2,1,0:T(2,128)(2,1)}), bf16[8,2,4096]{2,1,0:T(2,128)(2,1)S(1)}, u32[]{:S(2)}, u32[]{:S(2)}) async-start(bf16[8,2,4096]{2,1,0:T(2,128)(2,1)} %reshape.230), calls=%async_computation.2 | async-start | bytes 262144 | tf_op jit(solution)/shard_map/all_to_all | solution.py:54
  24.6 10.1 %all-to-all-start.1 = ((bf16[8,2,4096]{2,1,0:T(2,128)(2,1)}), bf16[8,2,4096]{2,1,0:T(2,128)(2,1)S(1)}, u32[]{:S(2)}, u32[]{:S(2)}) async-start(bf16[8,2,4096]{2,1,0:T(2,128)(2,1)} %reshape.232), calls=%async_computation.1 | async-start | bytes 262144 | tf_op jit(solution)/shard_map/all_to_all | solution.py:55
  34.7 10.1 %all-to-all-start = ((bf16[8,2,4096]{2,1,0:T(2,128)(2,1)}), bf16[8,2,4096]{2,1,0:T(2,128)(2,1)S(1)}, u32[]{:S(2)}, u32[]{:S(2)}) async-start(bf16[8,2,4096]{2,1,0:T(2,128)(2,1)} %reshape.234), calls=%async_computation | async-start | bytes 262144 | tf_op jit(solution)/shard_map/all_to_all | solution.py:56
  38.1 51.1 %all-reduce.3.cloned.1.call-start = ((), (), s32[]{:S(2)}) async-start(), calls=%async_computation.4 | async-start | bytes 524288 | tf_op jit(solution)/shard_map/psum | solution.py:16
  46.9 43.6 %copy-start.2 = (s32[1,512]{1,0:T(1,128)S(1)}, s32[1,512]{1,0:T(1,128)}, u32[]{:S(2)}) copy-start(s32[1,512]{1,0:T(1,128)} %param.8) | copy-start | bytes 6148
  90.9 0.9 copy-start.3
Sparse Core Ops, SparseCore 0:
  47.0 42.0 all-reduce.2
where the time goes:
time: 113 us
  waiting for transfers between devices  53.2 us (47%)
  between operations  14.3 us (13%)
  starting transfers between devices  13.1 us (12%)
  blocking collectives  11.2 us (10%)
  local copies, waits for them, and re-layouts  10.2 us (9%)
  other arithmetic  8.91 us (8%)
  matrix products  1.87 us (2%)
    psum x1, waiting for transfers between devices, broadcast(): return lax.psum(block, axis)  42.1 us
    all_to_all x1, blocking collectives, on_device(): lax.all_to_all(attended_heads[None], 'sp', split_axis=1, concat_axis=2, t...  11.2 us
    unnamed x4, other arithmetic  8.14 us
    unnamed x24, local copies, waits for them, and re-layouts  7 us
    all_to_all x1, starting transfers between devices, on_device(): lax.all_to_all(queries, 'sp', split_axis=2, concat_axis=1, tiled=True)  6.33 us
    all_to_all x1, waiting for transfers between devices, on_device(): lax.all_to_all(values, 'sp', split_axis=2, concat_axis=1, tiled=True)  5.95 us
    all_to_all x1, starting transfers between devices, on_device(): lax.all_to_all(values, 'sp', split_axis=2, concat_axis=1, tiled=True)  3.37 us
    all_to_all x1, starting transfers between devices, on_device(): lax.all_to_all(keys, 'sp', split_axis=2, concat_axis=1, tiled=True)  3.37 us
  transfers between devices with their start and end apart: 4, of which 4 were waited for; matrix products, arithmetic and copies ran while one was open for 8% of the time, Pallas kernels for 0%

commit v1 on v0

v1 whole, which is shorter than its diff:
```python
import math

import jax
import jax.numpy as jnp
from jax import lax
from jax.experimental import pallas as pl
from jax.experimental.pallas import tpu as pltpu
from jax.sharding import PartitionSpec as P

HD = 128
CORES = 2
NEG = -1e30
EXP_SCALE = 1.0 / (math.sqrt(HD) * math.log(2.0))
VMEM_LIMIT = 48 * 2**20
ANY = pl.BlockSpec(memory_space=pl.ANY)
SMEM = pl.BlockSpec(memory_space=pltpu.SMEM)


def in_vmem(count):
    return [pl.BlockSpec(memory_space=pltpu.VMEM)] * count


def resident(*arrays):
    return [pltpu.with_memory_space_constraint(x, pltpu.VMEM) for x in arrays]


def swap(x, flip):
    return lax.ppermute(x, "sp", [(i, i ^ flip) for i in range(lax.axis_size("sp"))])


def pack(queries, keys, values):
    chips = lax.axis_size("sp") // CORES
    rows, width = queries.shape[1], queries.shape[2] // chips

    def body(q_ref, k_ref, v_ref, *rest):
        qk_refs, v_refs, sems = rest[:chips], rest[chips : 2 * chips], rest[-1]
        chip = lax.axis_index("sp") // CORES
        copies = []
        for flip in reversed(range(chips)):
            columns = pl.ds(pl.multiple_of((chip ^ flip) * width, HD), width)
            targets = (qk_refs[flip].at[0], qk_refs[flip].at[1], v_refs[flip])
            for part, source in enumerate((q_ref, k_ref, v_ref)):
                copies.append(
                    pltpu.make_async_copy(
                        source.at[0, :, columns], targets[part], sems.at[3 * flip + part]
                    )
                )
        for copy in copies:
            copy.start()
        for copy in copies:
            copy.wait()

    outs = pl.pallas_call(
        body,
        out_shape=[pltpu.VMEM((2, rows, width), keys.dtype)] * chips
        + [pltpu.VMEM((rows, width), values.dtype)] * chips,
        in_specs=[ANY] * 3,
        out_specs=in_vmem(2 * chips),
        scratch_shapes=[pltpu.SemaphoreType.DMA((3 * chips,))],
        name="pack",
    )(queries, keys, values)
    return outs[:chips], outs[chips:]


def join(blocks, after=()):
    chips, parts = len(blocks), blocks[0].shape[:-2]
    rows, width = blocks[0].shape[-2:]
    count = parts[0] if parts else 1

    def body(*refs):
        for flip, block in zip(reversed(range(chips)), refs[:chips]):
            for part, out in enumerate(refs[chips + len(after) :]):
                out[chip_rows(flip, rows), :] = block[part] if parts else block[...]

    return pl.pallas_call(
        body,
        out_shape=[pltpu.VMEM((chips * rows, width), blocks[0].dtype)] * count,
        in_specs=in_vmem(chips + len(after)),
        out_specs=in_vmem(count),
        name="join",
    )(*resident(*reversed(blocks), *after))


def chip_rows(flip, rows):
    chip = lax.axis_index("sp") // CORES
    return pl.ds(pl.multiple_of((chip ^ flip) * rows, rows), rows)


def turn(x, bit):
    return lax.ppermute(x, "grp", [(i, i ^ (1 << bit)) for i in range(lax.axis_size("grp"))])


def choose(mine, theirs, anchor, bit, after=()):
    def body(anchor_ref, mine_ref, theirs_ref, *rest):
        out_ref = rest[-1]
        same = ((anchor_ref[0] % lax.axis_size("grp") ^ lax.axis_index("grp")) >> bit) & 1

        @pl.when(same == 0)
        def _():
            out_ref[...] = mine_ref[...]

        @pl.when(same != 0)
        def _():
            out_ref[...] = theirs_ref[...]

    return pl.pallas_call(
        body,
        out_shape=pltpu.VMEM(mine.shape, mine.dtype),
        in_specs=[SMEM] + in_vmem(2 + len(after)),
        out_specs=in_vmem(1)[0],
        name="choose",
    )(anchor, *resident(mine, theirs, *after))


def scores_of(q, k_ref, columns):
    return lax.dot_general(
        q, k_ref[:, columns], (((1,), (1,)), ((), ())), preferred_element_type=jnp.float32
    )


def mix(weights, v_ref, columns):
    return jnp.dot(
        weights.astype(jnp.bfloat16), v_ref[:, columns], preferred_element_type=jnp.float32
    )


def each_chunk(length, chunk):
    step = min(256, length)
    if length == step:
        chunk(0, step)
    else:
        pl.loop(0, length // step)(lambda index: chunk(pl.multiple_of(index * step, step), step))


def cost(length, width):
    return pl.CostEstimate(
        flops=8 * length * length * width,
        bytes_accessed=0,
        transcendentals=2 * length * length * (width // HD),
    )


def attend(q, own_k, own_v, other_k, other_v, columns, own_mask, other_mask, before):
    first = own_mask(scores_of(q, own_k, columns))
    second = other_mask(scores_of(q, other_k, columns))
    top = jnp.maximum(jnp.max(first, axis=1, keepdims=True), jnp.max(second, axis=1, keepdims=True))
    if before is not None:
        top = jnp.maximum(top, before[0])
    first = jnp.exp2((first - top) * EXP_SCALE)
    second = jnp.exp2((second - top) * EXP_SCALE)
    total = jnp.sum(first, axis=1, keepdims=True) + jnp.sum(second, axis=1, keepdims=True)
    acc = mix(first, own_v, columns) + mix(second, other_v, columns)
    if before is not None:
        keep = jnp.exp2((before[0] - top) * EXP_SCALE)
        total, acc = keep * before[1] + total, keep * before[2] + acc
    return top, total, acc


def near(q_rows, own, other, positions):
    length, width = q_rows.shape
    chips = lax.axis_size("sp") // CORES
    rows = length // chips
    paired = CORES * rows == HD and chips % 2 == 0
    if not paired:
        positions = jnp.swapaxes(positions.reshape(chips, CORES, rows), 0, 1).reshape(CORES, length)

    def split(at):
        if not paired:
            return [jnp.broadcast_to(at[c : c + 1, :], (8, length)) for c in range(CORES)]
        low = lax.broadcasted_iota(jnp.int32, (8, HD), 1) < rows
        tokens = [jnp.broadcast_to(at[:, c * HD : (c + 1) * HD], (8, HD)) for c in range(chips)]
        turned = [pltpu.roll(row, rows, 1) for row in tokens]
        pairs = range(0, chips, 2)
        return [
            jnp.concatenate([jnp.where(low, tokens[c], turned[c + 1]) for c in pairs], 1),
            jnp.concatenate([jnp.where(low, turned[c], tokens[c + 1]) for c in pairs], 1),
        ]

    def body(q_ref, own_k, own_v, other_k, other_v, at, top_ref, sum_ref, acc_ref, end_ref, own_at):
        end_ref[...] = jnp.zeros_like(end_ref)
        core = lax.axis_index("sp") % CORES
        first_at, second_at = split(at)
        own_at[...] = jnp.where(core == 0, first_at, second_at)
        other_at = jnp.where(core == 0, second_at, first_at)[:1, :]

        def chunk(start, step):
            here = pl.ds(start, step)
            order = jnp.transpose(jnp.broadcast_to(own_at[:1, here], (HD, step)))[:, :1]
            for head in range(width // HD):
                columns = slice(head * HD, (head + 1) * HD)
                top, total, acc = attend(
                    q_ref[here, columns],
                    own_k,
                    own_v,
                    other_k,
                    other_v,
                    columns,
                    lambda scores: jnp.where(own_at[:1, :] <= order, scores, NEG),
                    lambda scores: jnp.where(other_at <= order, scores, NEG),
                    None,
                )
                top_ref[head, here, :] = jnp.broadcast_to(top, (step, HD))
                sum_ref[head, here, :] = jnp.broadcast_to(total, (step, HD))
                acc_ref[here, columns] = acc

        each_chunk(length, chunk)

    state = pltpu.VMEM((width // HD, length, HD), jnp.float32)
    return pl.pallas_call(
        body,
        out_shape=[
            state,
            state,
            pltpu.VMEM((length, width), jnp.float32),
            pltpu.VMEM((8, HD), jnp.float32),
        ],
        in_specs=in_vmem(6),
        out_specs=in_vmem(4),
        scratch_shapes=[pltpu.VMEM((8, length), jnp.int32)],
        compiler_params=pltpu.CompilerParams(vmem_limit_bytes=VMEM_LIMIT),
        cost_estimate=cost(length, width),
        name="near",
    )(*resident(q_rows, *own, *other), positions)


def far(q_rows, state, own, other, anchor):
    length, width = q_rows.shape
    chips = lax.axis_size("sp") // CORES
    rows = length // chips

    def body(anchor_ref, q_ref, top_ref, sum_ref, acc_ref, own_k, own_v, other_k, other_v, *rest):
        out_refs, done = rest[:chips], rest[chips]
        hidden = lax.axis_index("grp") == anchor_ref[0] % lax.axis_size("grp")

        def mask(scores):
            return jnp.where(hidden, NEG, scores)

        def chunk(start, step):
            here = pl.ds(start, step)
            for head in range(width // HD):
                columns = slice(head * HD, (head + 1) * HD)
                before = (
                    top_ref[head, here, :][:, :1],
                    sum_ref[head, here, :][:, :1],
                    acc_ref[here, columns],
                )
                _, total, acc = attend(
                    q_ref[here, columns], own_k, own_v, other_k, other_v, columns, mask, mask, before
                )
                done[here, columns] = (acc / total).astype(jnp.bfloat16)

        each_chunk(length, chunk)
        for flip, out in zip(reversed(range(chips)), out_refs):
            out[...] = done[chip_rows(flip, rows), :]

    outs = pl.pallas_call(
        body,
        out_shape=[pltpu.VMEM((rows, width), jnp.bfloat16)] * chips,
        in_specs=[SMEM] + in_vmem(8),
        out_specs=in_vmem(chips),
        scratch_shapes=[pltpu.VMEM((length, width), jnp.bfloat16)],
        compiler_params=pltpu.CompilerParams(vmem_limit_bytes=VMEM_LIMIT),
        cost_estimate=cost(length, width),
        name="far",
    )(anchor, *resident(q_rows, *state, *own, *other))
    return outs[::-1]


def unpack(blocks):
    chips = len(blocks)
    rows, width = blocks[0].shape

    def body(*refs):
        block_refs, out_ref, sems = refs[:chips], refs[chips], refs[-1]
        chip = lax.axis_index("sp") // CORES
        copies = []
        for flip, block in zip(reversed(range(chips)), block_refs):
            columns = pl.ds(pl.multiple_of((chip ^ flip) * width, HD), width)
            copies.append(pltpu.make_async_copy(block, out_ref.at[0, :, columns], sems.at[flip]))
        for copy in copies:
            copy.start()
        for copy in copies:
            copy.wait()

    return pl.pallas_call(
        body,
        out_shape=jax.ShapeDtypeStruct((1, rows, chips * width), blocks[0].dtype),
        in_specs=in_vmem(chips),
        out_specs=ANY,
        scratch_shapes=[pltpu.SemaphoreType.DMA((chips,))],
        name="unpack",
    )(*resident(*reversed(blocks)))


def trade(blocks):
    moved = {flip: swap(blocks[flip], CORES * flip) for flip in reversed(range(1, len(blocks)))}
    return [blocks[0]] + [moved[flip] for flip in range(1, len(blocks))]


def on_device(queries, keys, values, positions, anchor):
    qk_blocks, v_blocks = pack(queries, keys, values)
    q_rows, k_own = join(trade(qk_blocks))
    (v_own,) = join(trade(v_blocks), [q_rows])
    own = k_own, v_own
    other = [swap(x, 1) for x in own]
    *state, end = near(q_rows, own, other, positions)

    bits = lax.axis_size("grp").bit_length() - 1
    k_far, v_far = own
    for stage in range(bits):
        after = [end] if stage == 1 else ()
        k_far = choose(k_far, turn(k_far, stage), anchor, stage, after)
        back = bits - 1 - stage
        v_far = choose(v_far, turn(v_far, back), anchor, back)
    other = [swap(x, 1) for x in (k_far, v_far)]
    return unpack(trade(far(q_rows, state, (k_far, v_far), other, anchor)))


def solution(mesh):
    return jax.shard_map(
        on_device,
        mesh=mesh,
        in_specs=(
            P("grp", "sp", None),
            P("grp", "sp", None),
            P("grp", "sp", None),
            P("grp", None),
            P(),
        ),
        out_specs=P("grp", "sp", None),
        check_vma=False,
    )
```

time: 113 us -> 36 us (0.32)
  waiting for transfers between devices: 53.2 us -> 10.1 us
  between operations: 14.3 us -> 0.76 us
  blocking collectives: 11.2 us -> 0 us
  local copies, waits for them, and re-layouts: 10.2 us -> 0.01 us
  other arithmetic: 8.91 us -> 0 us
  starting transfers between devices: 13.1 us -> 21.3 us
  Pallas kernels: 0 us -> 3.77 us
  matrix products: 1.87 us -> 0 us
    psum x1 -> x0, waiting for transfers between devices: 42.1 us -> none  [broadcast(): return lax.psum(block, axis)]
    ppermute x0 -> x17, starting transfers between devices: none -> 21.3 us  [the longest x13 15.4 us: swap(): lax.ppermute(x, 'sp', [(i, i ^ flip) for i in range(lax.axis_size('sp'))])]
    all_to_all x3 -> x0, starting transfers between devices: 13.1 us -> none  [the longest x1 6.33 us: on_device(): lax.all_to_all(queries, 'sp', split_axis=2, concat_axis=1, tiled=True)]
    all_to_all x1 -> x0, blocking collectives: 11.2 us -> none  [on_device(): lax.all_to_all(attended_heads[None], 'sp', split_axis=1, concat_axis=2, t...]
    all_to_all x3 -> x0, waiting for transfers between devices: 11 us -> none  [the longest x1 5.95 us: on_device(): lax.all_to_all(values, 'sp', split_axis=2, concat_axis=1, tiled=True)]
    ppermute x0 -> x17, waiting for transfers between devices: none -> 10.1 us  [the longest x13 6.63 us: swap(): lax.ppermute(x, 'sp', [(i, i ^ flip) for i in range(lax.axis_size('sp'))])]
    unnamed x4 -> x0, other arithmetic: 8.14 us -> none
    unnamed x24 -> x2, local copies, waits for them, and re-layouts: 7 us -> 0.01 us
  transfers between devices with their start and end apart: 4 -> 17, of which waited for: 4 -> 8; matrix products, arithmetic and copies ran while one was open for 8% -> 0% of each run, Pallas kernels for 0% -> 3%
where the time goes in v1:
time: 36 us; the launch traced here: 35.8 us
  starting transfers between devices  21.3 us (59%)
  waiting for transfers between devices  10.1 us (28%)
  Pallas kernels  3.77 us (10%)
  between operations  0.76 us (2%)
    ppermute x13, starting transfers between devices, swap(): lax.ppermute(x, 'sp', [(i, i ^ flip) for i in range(lax.axis_size('sp'))])  15.4 us
    ppermute x13, waiting for transfers between devices, swap(): lax.ppermute(x, 'sp', [(i, i ^ flip) for i in range(lax.axis_size('sp'))])  6.63 us
    ppermute x4, starting transfers between devices, turn(): lax.ppermute(x, 'grp', [(i, i ^ 1 << bit) for i in range(lax.axis_size('g...  5.83 us
    ppermute x4, waiting for transfers between devices, turn(): lax.ppermute(x, 'grp', [(i, i ^ 1 << bit) for i in range(lax.axis_size('g...  3.42 us
    pallas_call x1, Pallas kernels, pack(): pl.pallas_call(body, out_shape=[pltpu.VMEM((2, rows, width), keys.dtype)]...  1.04 us
    pallas_call x1, Pallas kernels, far(): pl.pallas_call(body, out_shape=[pltpu.VMEM((rows, width), jnp.bfloat16)]...  1 us
    pallas_call x1, Pallas kernels, near(): pl.pallas_call(body, out_shape=[state, state, pltpu.VMEM((length, width),...  0.94 us
  transfers between devices with their start and end apart: 17, of which 8 were waited for; matrix products, arithmetic and copies ran while one was open for 0% of the time, Pallas kernels for 3%

profile of v1, /device:TPU:0, one launch (start us, length us, event | category | flops | bytes accessed | tf_op | source)
XLA Modules:
  0.0 35.8 jit_solution(2634106985762802828)
XLA Ops:
  0.0 1.0 %pack.1 = (bf16[2,64,256]{2,1,0:T(8,128)(2,1)S(1)}, bf16[2,64,256]{2,1,0:T(8,128)(2,1)S(1)}, bf16[2,64,256]{2,1,0:T(8,128)(2,1)S(1)}, bf16[2,64,256]{2,1,0:T(8,1...) custom-call(bf16[1,64,1024]{2,1,0:T(8,128)(2,1)} %q_ref.1, ...), custom_call_target="tpu_custom_call" | custom-call | tf_op jit(solution)/shard_map/pack/pallas_call | solution.py:53
  1.0 5.1 %collective-permute-start = (bf16[2,64,256]{2,1,0:T(8,128)(2,1)S(1)}, bf16[2,64,256]{2,1,0:T(8,128)(2,1)S(1)}, u32[]{:S(2)}, u32[]{:S(2)}) collective-permute-start(bf16[2,64,256]{2,1,0:T(8,128)(2,1)S(1)} %get-tuple-element.23), channel_id=1, source_target_pairs={{0,6},{1,7},{2,4},{3,5},{4,2},{5,3},{6,0},{7,1},{8,14},{9,15},{10,... | collective-permute-start | bytes 196616 | tf_op jit(solution)/shard_map/ppermute | solution.py:28
  6.2 0.0 collective-permute-start.1
  6.2 0.6 %collective-permute-start.2 = (bf16[2,64,256]{2,1,0:T(8,128)(2,1)S(1)}, bf16[2,64,256]{2,1,0:T(8,128)(2,1)S(1)}, u32[]{:S(2)}, u32[]{:S(2)}) collective-permute-start(bf16[2,64,256]{2,1,0:T(8,128)(2,1)S(1)} %get-tuple-element.25), channel_id=1, source_target_pairs={{0,2},{1,3},{2,0},{3,1},{4,6},{5,7},{6,4},{7,5},{8,10},{9,11},{10,... | collective-permute-start | bytes 196616 | tf_op jit(solution)/shard_map/ppermute | solution.py:28
  6.8 3.7 %collective-permute-start.3 = (bf16[64,256]{1,0:T(8,128)(2,1)S(1)}, bf16[64,256]{1,0:T(8,128)(2,1)S(1)}, u32[]{:S(2)}, u32[]{:S(2)}) collective-permute-start(bf16[64,256]{1,0:T(8,128)(2,1)S(1)} %get-tuple-element.29), channel_id=1, source_target_pairs={{0,6},{1,7},{2,4},{3,5},{4,2},{5,3},{6,0},{7,1},{8,14},{9,15},{10,... | collective-permute-start | bytes 98312 | tf_op jit(solution)/shard_map/ppermute | solution.py:28
  10.6 0.0 collective-permute-start.4
  10.6 0.0 collective-permute-done.refs_0_
  10.6 0.8 %collective-permute-start.5 = (bf16[64,256]{1,0:T(8,128)(2,1)S(1)}, bf16[64,256]{1,0:T(8,128)(2,1)S(1)}, u32[]{:S(2)}, u32[]{:S(2)}) collective-permute-start(bf16[64,256]{1,0:T(8,128)(2,1)S(1)} %get-tuple-element.31), channel_id=1, source_target_pairs={{0,2},{1,3},{2,0},{3,1},{4,6},{5,7},{6,4},{7,5},{8,10},{9,11},{10,... | collective-permute-start | bytes 98312 | tf_op jit(solution)/shard_map/ppermute | solution.py:28
  11.4 1.5 %collective-permute-done.1.refs_1_ = bf16[2,64,256]{2,1,0:T(8,128)(2,1)S(1)} collective-permute-done((bf16[2,64,256]{2,1,0:T(8,128)(2,1)S(1)}, bf16[2,64,256]{2,1,0:T(8,128)(2,1)S(1)}, u32[]{:S(2)}, u32[]{:S(2)}) %collective-permute-start.1) | collective-permute-done | bytes 65568 | tf_op jit(solution)/shard_map/ppermute | solution.py:28
  12.8 0.0 collective-permute-done.2.refs_2_
  12.9 1.5 %collective-permute-start.8 = (bf16[256,256]{1,0:T(8,128)(2,1)S(1)}, bf16[256,256]{1,0:T(8,128)(2,1)S(1)}, u32[]{:S(2)}, u32[]{:S(2)}) collective-permute-start(bf16[256,256]{1,0:T(8,128)(2,1)S(1)} %get-tuple-element.28.own_k.mine_ref), channel_id=1, source_target_pairs={{0,8},{8,0},{16,24},{24,16},{1,9},{9,1},{17,25},{25,17},{2,10},{10... | collective-permute-start | bytes 393224 | tf_op jit(solution)/shard_map/ppermute | solution.py:90
  14.3 0.0 collective-permute-done.3.refs_0_
  14.3 1.0 %collective-permute-done.4.refs_1_ = bf16[64,256]{1,0:T(8,128)(2,1)S(1)} collective-permute-done((bf16[64,256]{1,0:T(8,128)(2,1)S(1)}, bf16[64,256]{1,0:T(8,128)(2,1)S(1)}, u32[]{:S(2)}, u32[]{:S(2)}) %collective-permute-start.4) | collective-permute-done | bytes 32800 | tf_op jit(solution)/shard_map/ppermute | solution.py:28
  15.4 0.0 collective-permute-done.5.refs_2_
  15.4 1.6 %collective-permute-start.10 = (bf16[256,256]{1,0:T(8,128)(2,1)S(1)}, bf16[256,256]{1,0:T(8,128)(2,1)S(1)}, u32[]{:S(2)}, u32[]{:S(2)}) collective-permute-start(bf16[256,256]{1,0:T(8,128)(2,1)S(1)} %join.3.own_v.mine_ref), channel_id=1, source_target_pairs={{0,16},{8,24},{16,0},{24,8},{1,17},{9,25},{17,1},{25,9},{2,18},{10... | collective-permute-start | bytes 393224 | tf_op jit(solution)/shard_map/ppermute | solution.py:90
  17.0 0.0 collective-permute-start.6
  17.0 0.5 %collective-permute-start.7 = (bf16[256,256]{1,0:T(8,128)(2,1)S(1)}, bf16[256,256]{1,0:T(8,128)(2,1)S(1)}, u32[]{:S(2)}, u32[]{:S(2)}) collective-permute-start(bf16[256,256]{1,0:T(8,128)(2,1)S(1)} %join.3.own_v.mine_ref), channel_id=1, source_target_pairs={{0,1},{1,0},{2,3},{3,2},{4,5},{5,4},{6,7},{7,6},{8,9},{9,8},{10,11... | collective-permute-start | bytes 393224 | tf_op jit(solution)/shard_map/ppermute | solution.py:28
  18.1 0.0 collective-permute-done.8.theirs_ref
  18.2 0.0 copy-start
  18.2 1.2 %collective-permute-start.9 = (bf16[256,256]{1,0:T(8,128)(2,1)S(1)}, bf16[256,256]{1,0:T(8,128)(2,1)S(1)}, u32[]{:S(2)}, u32[]{:S(2)}) collective-permute-start(bf16[256,256]{1,0:T(8,128)(2,1)S(1)} %choose.4.mine_ref), channel_id=1, source_target_pairs={{0,16},{8,24},{16,0},{24,8},{1,17},{9,25},{17,1},{25,9},{2,18},{10... | collective-permute-start | bytes 393224 | tf_op jit(solution)/shard_map/ppermute | solution.py:90
  19.4 1.0 %collective-permute-done.10.theirs_ref = bf16[256,256]{1,0:T(8,128)(2,1)S(1)} collective-permute-done((bf16[256,256]{1,0:T(8,128)(2,1)S(1)}, bf16[256,256]{1,0:T(8,128)(2,1)S(1)}, u32[]{:S(2)}, u32[]{:S(2)}) %collective-permute-start.10) | collective-permute-done | bytes 131104 | tf_op jit(solution)/shard_map/ppermute | solution.py:90
  20.4 1.6 %collective-permute-start.11 = (bf16[256,256]{1,0:T(8,128)(2,1)S(1)}, bf16[256,256]{1,0:T(8,128)(2,1)S(1)}, u32[]{:S(2)}, u32[]{:S(2)}) collective-permute-start(bf16[256,256]{1,0:T(8,128)(2,1)S(1)} %choose.6.mine_ref), channel_id=1, source_target_pairs={{0,8},{8,0},{16,24},{24,16},{1,9},{9,1},{17,25},{25,17},{2,10},{10... | collective-permute-start | bytes 393224 | tf_op jit(solution)/shard_map/ppermute | solution.py:90
  22.0 0.0 collective-permute-done.6.other_k
  22.0 0.0 collective-permute-done.7.other_v
  22.0 0.0 copy-done
  22.0 0.9 %near.1 = (f32[2,256,128]{2,1,0:T(8,128)S(1)}, f32[2,256,128]{2,1,0:T(8,128)S(1)}, f32[256,256]{1,0:T(8,128)S(1)}, f32[8,128]{1,0:T(8,128)S(1)}) custom-call(bf16[256,256]{1,0:T(8,128)(2,1)S(1)} %get-tuple-element.27.refs_4_.q_ref, bf16[256,256]{1,0:T(8,128)(2,1)S(1)} %get-tuple-element.28.own_k.mine_ref, bf16[256,256]{1,0:T(8,128)(2,1)S(1)} %join.3.own_v.mine_ref, ...), custom_call_target="tpu_custom_call" | custom-call | flops 134217728 | tf_op jit(solution)/shard_map/near/pallas_call | solution.py:209
  23.0 0.7 %collective-permute-done.9.theirs_ref = bf16[256,256]{1,0:T(8,128)(2,1)S(1)} collective-permute-done((bf16[256,256]{1,0:T(8,128)(2,1)S(1)}, bf16[256,256]{1,0:T(8,128)(2,1)S(1)}, u32[]{:S(2)}, u32[]{:S(2)}) %collective-permute-start.9) | collective-permute-done | bytes 131104 | tf_op jit(solution)/shard_map/ppermute | solution.py:90
  23.7 0.1 collective-permute-start.12
  23.8 1.7 %collective-permute-done.11.theirs_ref = bf16[256,256]{1,0:T(8,128)(2,1)S(1)} collective-permute-done((bf16[256,256]{1,0:T(8,128)(2,1)S(1)}, bf16[256,256]{1,0:T(8,128)(2,1)S(1)}, u32[]{:S(2)}, u32[]{:S(2)}) %collective-permute-start.11) | collective-permute-done | bytes 131104 | tf_op jit(solution)/shard_map/ppermute | solution.py:90
  25.5 0.1 collective-permute-start.13
  25.6 0.0 collective-permute-done.12.other_k
  25.6 1.3 %collective-permute-done.13.other_v = bf16[256,256]{1,0:T(8,128)(2,1)S(1)} collective-permute-done((bf16[256,256]{1,0:T(8,128)(2,1)S(1)}, bf16[256,256]{1,0:T(8,128)(2,1)S(1)}, u32[]{:S(2)}, u32[]{:S(2)}) %collective-permute-start.13) | collective-permute-done | bytes 131104 | tf_op jit(solution)/shard_map/ppermute | solution.py:28
  26.9 1.0 %far.1 = (bf16[64,256]{1,0:T(8,128)(2,1)S(1)}, bf16[64,256]{1,0:T(8,128)(2,1)S(1)}, bf16[64,256]{1,0:T(8,128)(2,1)S(1)}, bf16[64,256]{1,0:T(8,128)(2,1)S(1)}) custom-call(s32[1]{0:T(128)S(6)} %copy.6.anchor_ref, bf16[256,256]{1,0:T(8,128)(2,1)S(1)} %get-tuple-element.27.refs_4_.q_ref, f32[2,256,128]{2,1,0:T(8,128)S(1)} %get-tuple-element.33.top_ref, ...), custom_call_target="tpu_custom_call" | custom-call | flops 134217728 | tf_op jit(solution)/shard_map/far/pallas_call | solution.py:256
  27.9 2.2 %collective-permute-start.14 = (bf16[64,256]{1,0:T(8,128)(2,1)S(1)}, bf16[64,256]{1,0:T(8,128)(2,1)S(1)}, u32[]{:S(2)}, u32[]{:S(2)}) collective-permute-start(bf16[64,256]{1,0:T(8,128)(2,1)S(1)} %get-tuple-element.37), channel_id=1, source_target_pairs={{0,6},{1,7},{2,4},{3,5},{4,2},{5,3},{6,0},{7,1},{8,14},{9,15},{10,... | collective-permute-start | bytes 98312 | tf_op jit(solution)/shard_map/ppermute | solution.py:28
  30.1 0.0 collective-permute-start.15
  30.1 2.2 %collective-permute-start.16 = (bf16[64,256]{1,0:T(8,128)(2,1)S(1)}, bf16[64,256]{1,0:T(8,128)(2,1)S(1)}, u32[]{:S(2)}, u32[]{:S(2)}) collective-permute-start(bf16[64,256]{1,0:T(8,128)(2,1)S(1)} %get-tuple-element.39), channel_id=1, source_target_pairs={{0,2},{1,3},{2,0},{3,1},{4,6},{5,7},{6,4},{7,5},{8,10},{9,11},{10,... | collective-permute-start | bytes 98312 | tf_op jit(solution)/shard_map/ppermute | solution.py:28
  32.4 1.7 %collective-permute-done.14.refs_0_ = bf16[64,256]{1,0:T(8,128)(2,1)S(1)} collective-permute-done((bf16[64,256]{1,0:T(8,128)(2,1)S(1)}, bf16[64,256]{1,0:T(8,128)(2,1)S(1)}, u32[]{:S(2)}, u32[]{:S(2)}) %collective-permute-start.14) | collective-permute-done | bytes 32800 | tf_op jit(solution)/shard_map/ppermute | solution.py:28
  34.1 1.0 %collective-permute-done.15.refs_1_ = bf16[64,256]{1,0:T(8,128)(2,1)S(1)} collective-permute-done((bf16[64,256]{1,0:T(8,128)(2,1)S(1)}, bf16[64,256]{1,0:T(8,128)(2,1)S(1)}, u32[]{:S(2)}, u32[]{:S(2)}) %collective-permute-start.15) | collective-permute-done | bytes 32800 | tf_op jit(solution)/shard_map/ppermute | solution.py:28
  35.2 0.0 collective-permute-done.16.refs_2_
  35.2 0.7 %unpack.1 = bf16[1,64,1024]{2,1,0:T(8,128)(2,1)} custom-call(bf16[64,256]{1,0:T(8,128)(2,1)S(1)} %collective-permute-done.14.refs_0_, bf16[64,256]{1,0:T(8,128)(2,1)S(1)} %collective-permute-done.15.refs_1_, bf16[64,256]{1,0:T(8,128)(2,1)S(1)} %collective-permute-done.16.refs_2_, bf16[64,256]{1,0:T(8,128)(2,1)S(1)} %get-tuple-element.40.refs_3_), custom_call_target="tpu_custom_call" | custom-call | tf_op jit(solution)/shard_map/unpack/pallas_call | solution.py:285
  (6 shorter events, 0.1 us)
Async XLA Ops:
  1.0 9.5 %collective-permute-start = (bf16[2,64,256]{2,1,0:T(8,128)(2,1)S(1)}, bf16[2,64,256]{2,1,0:T(8,128)(2,1)S(1)}, u32[]{:S(2)}, u32[]{:S(2)}) collective-permute-start(bf16[2,64,256]{2,1,0:T(8,128)(2,1)S(1)} %get-tuple-element.23), channel_id=1, source_target_pairs={{0,6},{1,7},{2,4},{3,5},{4,2},{5,3},{6,0},{7,1},{8,14},{9,15},{10,... | collective-permute-start | bytes 196616 | tf_op jit(solution)/shard_map/ppermute | solution.py:28
  6.2 6.7 %collective-permute-start.1 = (bf16[2,64,256]{2,1,0:T(8,128)(2,1)S(1)}, bf16[2,64,256]{2,1,0:T(8,128)(2,1)S(1)}, u32[]{:S(2)}, u32[]{:S(2)}) collective-permute-start(bf16[2,64,256]{2,1,0:T(8,128)(2,1)S(1)} %get-tuple-element.24), channel_id=1, source_target_pairs={{0,4},{1,5},{2,6},{3,7},{4,0},{5,1},{6,2},{7,3},{8,12},{9,13},{10,... | collective-permute-start | bytes 196616 | tf_op jit(solution)/shard_map/ppermute | solution.py:28
  6.2 6.7 %collective-permute-start.2 = (bf16[2,64,256]{2,1,0:T(8,128)(2,1)S(1)}, bf16[2,64,256]{2,1,0:T(8,128)(2,1)S(1)}, u32[]{:S(2)}, u32[]{:S(2)}) collective-permute-start(bf16[2,64,256]{2,1,0:T(8,128)(2,1)S(1)} %get-tuple-element.25), channel_id=1, source_target_pairs={{0,2},{1,3},{2,0},{3,1},{4,6},{5,7},{6,4},{7,5},{8,10},{9,11},{10,... | collective-permute-start | bytes 196616 | tf_op jit(solution)/shard_map/ppermute | solution.py:28
  6.8 7.5 %collective-permute-start.3 = (bf16[64,256]{1,0:T(8,128)(2,1)S(1)}, bf16[64,256]{1,0:T(8,128)(2,1)S(1)}, u32[]{:S(2)}, u32[]{:S(2)}) collective-permute-start(bf16[64,256]{1,0:T(8,128)(2,1)S(1)} %get-tuple-element.29), channel_id=1, source_target_pairs={{0,6},{1,7},{2,4},{3,5},{4,2},{5,3},{6,0},{7,1},{8,14},{9,15},{10,... | collective-permute-start | bytes 98312 | tf_op jit(solution)/shard_map/ppermute | solution.py:28
  10.6 4.8 %collective-permute-start.4 = (bf16[64,256]{1,0:T(8,128)(2,1)S(1)}, bf16[64,256]{1,0:T(8,128)(2,1)S(1)}, u32[]{:S(2)}, u32[]{:S(2)}) collective-permute-start(bf16[64,256]{1,0:T(8,128)(2,1)S(1)} %get-tuple-element.30), channel_id=1, source_target_pairs={{0,4},{1,5},{2,6},{3,7},{4,0},{5,1},{6,2},{7,3},{8,12},{9,13},{10,... | collective-permute-start | bytes 98312 | tf_op jit(solution)/shard_map/ppermute | solution.py:28
  10.6 4.8 %collective-permute-start.5 = (bf16[64,256]{1,0:T(8,128)(2,1)S(1)}, bf16[64,256]{1,0:T(8,128)(2,1)S(1)}, u32[]{:S(2)}, u32[]{:S(2)}) collective-permute-start(bf16[64,256]{1,0:T(8,128)(2,1)S(1)} %get-tuple-element.31), channel_id=1, source_target_pairs={{0,2},{1,3},{2,0},{3,1},{4,6},{5,7},{6,4},{7,5},{8,10},{9,11},{10,... | collective-permute-start | bytes 98312 | tf_op jit(solution)/shard_map/ppermute | solution.py:28
  12.9 5.3 %collective-permute-start.8 = (bf16[256,256]{1,0:T(8,128)(2,1)S(1)}, bf16[256,256]{1,0:T(8,128)(2,1)S(1)}, u32[]{:S(2)}, u32[]{:S(2)}) collective-permute-start(bf16[256,256]{1,0:T(8,128)(2,1)S(1)} %get-tuple-element.28.own_k.mine_ref), channel_id=1, source_target_pairs={{0,8},{8,0},{16,24},{24,16},{1,9},{9,1},{17,25},{25,17},{2,10},{10... | collective-permute-start | bytes 393224 | tf_op jit(solution)/shard_map/ppermute | solution.py:90
  15.4 5.0 %collective-permute-start.10 = (bf16[256,256]{1,0:T(8,128)(2,1)S(1)}, bf16[256,256]{1,0:T(8,128)(2,1)S(1)}, u32[]{:S(2)}, u32[]{:S(2)}) collective-permute-start(bf16[256,256]{1,0:T(8,128)(2,1)S(1)} %join.3.own_v.mine_ref), channel_id=1, source_target_pairs={{0,16},{8,24},{16,0},{24,8},{1,17},{9,25},{17,1},{25,9},{2,18},{10... | collective-permute-start | bytes 393224 | tf_op jit(solution)/shard_map/ppermute | solution.py:90
  17.0 5.0 %collective-permute-start.6 = (bf16[256,256]{1,0:T(8,128)(2,1)S(1)}, bf16[256,256]{1,0:T(8,128)(2,1)S(1)}, u32[]{:S(2)}, u32[]{:S(2)}) collective-permute-start(bf16[256,256]{1,0:T(8,128)(2,1)S(1)} %get-tuple-element.28.own_k.mine_ref), channel_id=1, source_target_pairs={{0,1},{1,0},{2,3},{3,2},{4,5},{5,4},{6,7},{7,6},{8,9},{9,8},{10,11... | collective-permute-start | bytes 393224 | tf_op jit(solution)/shard_map/ppermute | solution.py:28
  17.0 5.0 %collective-permute-start.7 = (bf16[256,256]{1,0:T(8,128)(2,1)S(1)}, bf16[256,256]{1,0:T(8,128)(2,1)S(1)}, u32[]{:S(2)}, u32[]{:S(2)}) collective-permute-start(bf16[256,256]{1,0:T(8,128)(2,1)S(1)} %join.3.own_v.mine_ref), channel_id=1, source_target_pairs={{0,1},{1,0},{2,3},{3,2},{4,5},{5,4},{6,7},{7,6},{8,9},{9,8},{10,11... | collective-permute-start | bytes 393224 | tf_op jit(solution)/shard_map/ppermute | solution.py:28
  18.2 3.8 %copy-start = (s32[1,512]{1,0:T(1,128)S(1)}, s32[1,512]{1,0:T(1,128)}, u32[]{:S(2)}) copy-start(s32[1,512]{1,0:T(1,128)} %at.1) | copy-start | bytes 6148
  18.2 5.5 %collective-permute-start.9 = (bf16[256,256]{1,0:T(8,128)(2,1)S(1)}, bf16[256,256]{1,0:T(8,128)(2,1)S(1)}, u32[]{:S(2)}, u32[]{:S(2)}) collective-permute-start(bf16[256,256]{1,0:T(8,128)(2,1)S(1)} %choose.4.mine_ref), channel_id=1, source_target_pairs={{0,16},{8,24},{16,0},{24,8},{1,17},{9,25},{17,1},{25,9},{2,18},{10... | collective-permute-start | bytes 393224 | tf_op jit(solution)/shard_map/ppermute | solution.py:90
  20.4 5.0 %collective-permute-start.11 = (bf16[256,256]{1,0:T(8,128)(2,1)S(1)}, bf16[256,256]{1,0:T(8,128)(2,1)S(1)}, u32[]{:S(2)}, u32[]{:S(2)}) collective-permute-start(bf16[256,256]{1,0:T(8,128)(2,1)S(1)} %choose.6.mine_ref), channel_id=1, source_target_pairs={{0,8},{8,0},{16,24},{24,16},{1,9},{9,1},{17,25},{25,17},{2,10},{10... | collective-permute-start | bytes 393224 | tf_op jit(solution)/shard_map/ppermute | solution.py:90
  23.7 1.9 %collective-permute-start.12 = (bf16[256,256]{1,0:T(8,128)(2,1)S(1)}, bf16[256,256]{1,0:T(8,128)(2,1)S(1)}, u32[]{:S(2)}, u32[]{:S(2)}) collective-permute-start(bf16[256,256]{1,0:T(8,128)(2,1)S(1)} %choose.5.own_k), channel_id=1, source_target_pairs={{0,1},{1,0},{2,3},{3,2},{4,5},{5,4},{6,7},{7,6},{8,9},{9,8},{10,11... | collective-permute-start | bytes 393224 | tf_op jit(solution)/shard_map/ppermute | solution.py:28
  25.5 1.4 %collective-permute-start.13 = (bf16[256,256]{1,0:T(8,128)(2,1)S(1)}, bf16[256,256]{1,0:T(8,128)(2,1)S(1)}, u32[]{:S(2)}, u32[]{:S(2)}) collective-permute-start(bf16[256,256]{1,0:T(8,128)(2,1)S(1)} %choose.7.own_v), channel_id=1, source_target_pairs={{0,1},{1,0},{2,3},{3,2},{4,5},{5,4},{6,7},{7,6},{8,9},{9,8},{10,11... | collective-permute-start | bytes 393224 | tf_op jit(solution)/shard_map/ppermute | solution.py:28
  27.9 6.2 %collective-permute-start.14 = (bf16[64,256]{1,0:T(8,128)(2,1)S(1)}, bf16[64,256]{1,0:T(8,128)(2,1)S(1)}, u32[]{:S(2)}, u32[]{:S(2)}) collective-permute-start(bf16[64,256]{1,0:T(8,128)(2,1)S(1)} %get-tuple-element.37), channel_id=1, source_target_pairs={{0,6},{1,7},{2,4},{3,5},{4,2},{5,3},{6,0},{7,1},{8,14},{9,15},{10,... | collective-permute-start | bytes 98312 | tf_op jit(solution)/shard_map/ppermute | solution.py:28
  30.1 5.0 %collective-permute-start.15 = (bf16[64,256]{1,0:T(8,128)(2,1)S(1)}, bf16[64,256]{1,0:T(8,128)(2,1)S(1)}, u32[]{:S(2)}, u32[]{:S(2)}) collective-permute-start(bf16[64,256]{1,0:T(8,128)(2,1)S(1)} %get-tuple-element.38), channel_id=1, source_target_pairs={{0,4},{1,5},{2,6},{3,7},{4,0},{5,1},{6,2},{7,3},{8,12},{9,13},{10,... | collective-permute-start | bytes 98312 | tf_op jit(solution)/shard_map/ppermute | solution.py:28
  30.1 5.0 %collective-permute-start.16 = (bf16[64,256]{1,0:T(8,128)(2,1)S(1)}, bf16[64,256]{1,0:T(8,128)(2,1)S(1)}, u32[]{:S(2)}, u32[]{:S(2)}) collective-permute-start(bf16[64,256]{1,0:T(8,128)(2,1)S(1)} %get-tuple-element.39), channel_id=1, source_target_pairs={{0,2},{1,3},{2,0},{3,1},{4,6},{5,7},{6,4},{7,5},{8,10},{9,11},{10,... | collective-permute-start | bytes 98312 | tf_op jit(solution)/shard_map/ppermute | solution.py:28

commit v2 on v1

--- a/solution.py
+++ b/solution.py
@@ -62,13 +62,13 @@
     return outs[:chips], outs[chips:]
 
 
-def join(blocks, after=()):
+def join(blocks, order, after=()):
     chips, parts = len(blocks), blocks[0].shape[:-2]
     rows, width = blocks[0].shape[-2:]
     count = parts[0] if parts else 1
 
     def body(*refs):
-        for flip, block in zip(reversed(range(chips)), refs[:chips]):
+        for flip, block in zip((*order, 0), refs[:chips]):
             for part, out in enumerate(refs[chips + len(after) :]):
                 out[chip_rows(flip, rows), :] = block[part] if parts else block[...]
 
@@ -78,7 +78,7 @@
         in_specs=in_vmem(chips + len(after)),
         out_specs=in_vmem(count),
         name="join",
-    )(*resident(*reversed(blocks), *after))
+    )(*resident(*[blocks[flip] for flip in (*order, 0)], *after))
 
 
 def chip_rows(flip, rows):
@@ -119,9 +119,7 @@
 
 
 def mix(weights, v_ref, columns):
-    return jnp.dot(
-        weights.astype(jnp.bfloat16), v_ref[:, columns], preferred_element_type=jnp.float32
-    )
+    return jnp.dot(weights, v_ref[:, columns], preferred_element_type=jnp.float32)
 
 
 def each_chunk(length, chunk):
@@ -140,20 +138,16 @@
     )
 
 
-def attend(q, own_k, own_v, other_k, other_v, columns, own_mask, other_mask, before):
+def weigh(q, own_k, other_k, columns, own_mask, other_mask, before=None):
     first = own_mask(scores_of(q, own_k, columns))
     second = other_mask(scores_of(q, other_k, columns))
     top = jnp.maximum(jnp.max(first, axis=1, keepdims=True), jnp.max(second, axis=1, keepdims=True))
     if before is not None:
-        top = jnp.maximum(top, before[0])
+        top = jnp.maximum(top, before)
     first = jnp.exp2((first - top) * EXP_SCALE)
     second = jnp.exp2((second - top) * EXP_SCALE)
     total = jnp.sum(first, axis=1, keepdims=True) + jnp.sum(second, axis=1, keepdims=True)
-    acc = mix(first, own_v, columns) + mix(second, other_v, columns)
-    if before is not None:
-        keep = jnp.exp2((before[0] - top) * EXP_SCALE)
-        total, acc = keep * before[1] + total, keep * before[2] + acc
-    return top, total, acc
+    return first.astype(jnp.bfloat16), second.astype(jnp.bfloat16), top, total
 
 
 def near(q_rows, own, other, positions):
@@ -188,20 +182,17 @@
             order = jnp.transpose(jnp.broadcast_to(own_at[:1, here], (HD, step)))[:, :1]
             for head in range(width // HD):
                 columns = slice(head * HD, (head + 1) * HD)
-                top, total, acc = attend(
+                first, second, top, total = weigh(
                     q_ref[here, columns],
                     own_k,
-                    own_v,
                     other_k,
-                    other_v,
                     columns,
                     lambda scores: jnp.where(own_at[:1, :] <= order, scores, NEG),
                     lambda scores: jnp.where(other_at <= order, scores, NEG),
-                    None,
                 )
                 top_ref[head, here, :] = jnp.broadcast_to(top, (step, HD))
                 sum_ref[head, here, :] = jnp.broadcast_to(total, (step, HD))
-                acc_ref[here, columns] = acc
+                acc_ref[here, columns] = mix(first, own_v, columns) + mix(second, other_v, columns)
 
         each_chunk(length, chunk)
 
@@ -223,50 +214,83 @@
     )(*resident(q_rows, *own, *other), positions)
 
 
-def far(q_rows, state, own, other, anchor):
+def far_weights(q_rows, top, own_k, other_k, anchor):
     length, width = q_rows.shape
+    heads = width // HD
+
+    def body(anchor_ref, q_ref, old_ref, own_k, other_k, first_ref, second_ref, top_ref, sum_ref):
+        hidden = lax.axis_index("grp") == anchor_ref[0] % lax.axis_size("grp")
+
+        def mask(scores):
+            return jnp.where(hidden, NEG, scores)
+
+        def chunk(start, step):
+            here = pl.ds(start, step)
+            for head in range(heads):
+                columns = slice(head * HD, (head + 1) * HD)
+                old = old_ref[head, here, :][:, :1]
+                first, second, top, total = weigh(
+                    q_ref[here, columns], own_k, other_k, columns, mask, mask, old
+                )
+                first_ref[head, here, :] = first
+                second_ref[head, here, :] = second
+                top_ref[head, here, :] = jnp.broadcast_to(top, (step, HD))
+                sum_ref[head, here, :] = jnp.broadcast_to(total, (step, HD))
+
+        each_chunk(length, chunk)
+
+    weights = pltpu.VMEM((heads, length, length), jnp.bfloat16)
+    state = pltpu.VMEM((heads, length, HD), jnp.float32)
+    return pl.pallas_call(
+        body,
+        out_shape=[weights, weights, state, state],
+        in_specs=[SMEM] + in_vmem(4),
+        out_specs=in_vmem(4),
+        compiler_params=pltpu.CompilerParams(vmem_limit_bytes=VMEM_LIMIT),
+        cost_estimate=cost(length, width),
+        name="far_weights",
+    )(anchor, *resident(q_rows, top, own_k, other_k))
+
+
+def far_values(near_state, far_state, own_v, other_v):
+    length, width = near_state[-1].shape
     chips = lax.axis_size("sp") // CORES
     rows = length // chips
 
-    def body(anchor_ref, q_ref, top_ref, sum_ref, acc_ref, own_k, own_v, other_k, other_v, *rest):
-        out_refs, done = rest[:chips], rest[chips]
-        hidden = lax.axis_index("grp") == anchor_ref[0] % lax.axis_size("grp")
-
-        def mask(scores):
-            return jnp.where(hidden, NEG, scores)
+    def body(*refs):
+        old_top, old_sum, old_acc, first_ref, second_ref, top_ref, sum_ref, own_v, other_v = refs[:9]
+        out_refs, done = refs[9:-1], refs[-1]
 
         def chunk(start, step):
             here = pl.ds(start, step)
             for head in range(width // HD):
                 columns = slice(head * HD, (head + 1) * HD)
-                before = (
-                    top_ref[head, here, :][:, :1],
-                    sum_ref[head, here, :][:, :1],
-                    acc_ref[here, columns],
-                )
-                _, total, acc = attend(
-                    q_ref[here, columns], own_k, own_v, other_k, other_v, columns, mask, mask, before
+                keep = jnp.exp2((old_top[head, here, :] - top_ref[head, here, :]) * EXP_SCALE)
+                total = keep * old_sum[head, here, :] + sum_ref[head, here, :]
+                acc = (
+                    keep * old_acc[here, columns]
+                    + mix(first_ref[head, here, :], own_v, columns)
+                    + mix(second_ref[head, here, :], other_v, columns)
                 )
                 done[here, columns] = (acc / total).astype(jnp.bfloat16)
 
         each_chunk(length, chunk)
-        for flip, out in zip(reversed(range(chips)), out_refs):
+        for flip, out in enumerate(out_refs):
             out[...] = done[chip_rows(flip, rows), :]
 
-    outs = pl.pallas_call(
+    return pl.pallas_call(
         body,
         out_shape=[pltpu.VMEM((rows, width), jnp.bfloat16)] * chips,
-        in_specs=[SMEM] + in_vmem(8),
+        in_specs=in_vmem(9),
         out_specs=in_vmem(chips),
         scratch_shapes=[pltpu.VMEM((length, width), jnp.bfloat16)],
         compiler_params=pltpu.CompilerParams(vmem_limit_bytes=VMEM_LIMIT),
         cost_estimate=cost(length, width),
-        name="far",
-    )(anchor, *resident(q_rows, *state, *own, *other))
-    return outs[::-1]
-
-
-def unpack(blocks):
+        name="far_values",
+    )(*resident(*near_state, *far_state, own_v, other_v))
+
+
+def unpack(blocks, order):
     chips = len(blocks)
     rows, width = blocks[0].shape
 
@@ -274,7 +298,7 @@
         block_refs, out_ref, sems = refs[:chips], refs[chips], refs[-1]
         chip = lax.axis_index("sp") // CORES
         copies = []
-        for flip, block in zip(reversed(range(chips)), block_refs):
+        for flip, block in zip((*order, 0), block_refs):
             columns = pl.ds(pl.multiple_of((chip ^ flip) * width, HD), width)
             copies.append(pltpu.make_async_copy(block, out_ref.at[0, :, columns], sems.at[flip]))
         for copy in copies:
@@ -289,18 +313,19 @@
         out_specs=ANY,
         scratch_shapes=[pltpu.SemaphoreType.DMA((chips,))],
         name="unpack",
-    )(*resident(*reversed(blocks)))
-
-
-def trade(blocks):
-    moved = {flip: swap(blocks[flip], CORES * flip) for flip in reversed(range(1, len(blocks)))}
+    )(*resident(*[blocks[flip] for flip in (*order, 0)]))
+
+
+def trade(blocks, order):
+    moved = {flip: swap(blocks[flip], CORES * flip) for flip in order}
     return [blocks[0]] + [moved[flip] for flip in range(1, len(blocks))]
 
 
 def on_device(queries, keys, values, positions, anchor):
+    order = tuple(reversed(range(1, lax.axis_size("sp") // CORES)))
     qk_blocks, v_blocks = pack(queries, keys, values)
-    q_rows, k_own = join(trade(qk_blocks))
-    (v_own,) = join(trade(v_blocks), [q_rows])
+    q_rows, k_own = join(trade(qk_blocks, order), order)
+    (v_own,) = join(trade(v_blocks, order), order, [q_rows])
     own = k_own, v_own
     other = [swap(x, 1) for x in own]
     *state, end = near(q_rows, own, other, positions)
@@ -312,8 +337,9 @@
         k_far = choose(k_far, turn(k_far, stage), anchor, stage, after)
         back = bits - 1 - stage
         v_far = choose(v_far, turn(v_far, back), anchor, back)
-    other = [swap(x, 1) for x in (k_far, v_far)]
-    return unpack(trade(far(q_rows, state, (k_far, v_far), other, anchor)))
+    far_state = far_weights(q_rows, state[0], k_far, swap(k_far, 1), anchor)
+    done = far_values(state, far_state, v_far, swap(v_far, 1))
+    return unpack(trade(done, order), order)
 
 
 def solution(mesh):

time: 36 us -> 35.3 us (0.981)
  waiting for transfers between devices: 10.1 us -> 8.79 us
  Pallas kernels: 3.77 us -> 4.32 us
    ppermute x13, waiting for transfers between devices: 6.63 us -> 5.37 us  [swap(): lax.ppermute(x, 'sp', [(i, i ^ flip) for i in range(lax.axis_size('sp'))])]
    pallas_call x1 -> x2, Pallas kernels: 1 us -> 1.55 us  [the longest x1 1.26 us: far_weights(): pl.pallas_call(body, out_shape=[weights, weights, state, state], in_specs...]
  transfers between devices with their start and end apart: 17 -> 17, of which waited for: 8 -> 8; matrix products, arithmetic and copies ran while one was open for 0% -> 0% of each run, Pallas kernels for 3% -> 7%
where the time goes in v2:
time: 35.3 us; the launch traced here: 35.1 us
  starting transfers between devices  21.3 us (60%)
  waiting for transfers between devices  8.79 us (25%)
  Pallas kernels  4.32 us (12%)
  between operations  0.77 us (2%)
    ppermute x13, starting transfers between devices, swap(): lax.ppermute(x, 'sp', [(i, i ^ flip) for i in range(lax.axis_size('sp'))])  15.4 us
    ppermute x4, starting transfers between devices, turn(): lax.ppermute(x, 'grp', [(i, i ^ 1 << bit) for i in range(lax.axis_size('g...  5.84 us
    ppermute x13, waiting for transfers between devices, swap(): lax.ppermute(x, 'sp', [(i, i ^ flip) for i in range(lax.axis_size('sp'))])  5.37 us
    ppermute x4, waiting for transfers between devices, turn(): lax.ppermute(x, 'grp', [(i, i ^ 1 << bit) for i in range(lax.axis_size('g...  3.42 us
    pallas_call x1, Pallas kernels, far_weights(): pl.pallas_call(body, out_shape=[weights, weights, state, state], in_specs...  1.26 us
    pallas_call x1, Pallas kernels, pack(): pl.pallas_call(body, out_shape=[pltpu.VMEM((2, rows, width), keys.dtype)]...  1.04 us
    pallas_call x1, Pallas kernels, near(): pl.pallas_call(body, out_shape=[state, state, pltpu.VMEM((length, width),...  0.94 us
  transfers between devices with their start and end apart: 17, of which 8 were waited for; matrix products, arithmetic and copies ran while one was open for 0% of the time, Pallas kernels for 7%

profile of v2, /device:TPU:0, one launch (start us, length us, event | category | flops | bytes accessed | tf_op | source)
XLA Modules:
  0.0 35.1 jit_solution(4106402193731117141)
XLA Ops:
  0.0 1.0 %pack.1 = (bf16[2,64,256]{2,1,0:T(8,128)(2,1)S(1)}, bf16[2,64,256]{2,1,0:T(8,128)(2,1)S(1)}, bf16[2,64,256]{2,1,0:T(8,128)(2,1)S(1)}, bf16[2,64,256]{2,1,0:T(8,1...) custom-call(bf16[1,64,1024]{2,1,0:T(8,128)(2,1)} %q_ref.1, ...), custom_call_target="tpu_custom_call" | custom-call | tf_op jit(solution)/shard_map/pack/pallas_call | solution.py:53
  1.0 5.1 %collective-permute-start = (bf16[2,64,256]{2,1,0:T(8,128)(2,1)S(1)}, bf16[2,64,256]{2,1,0:T(8,128)(2,1)S(1)}, u32[]{:S(2)}, u32[]{:S(2)}) collective-permute-start(bf16[2,64,256]{2,1,0:T(8,128)(2,1)S(1)} %get-tuple-element.27), channel_id=1, source_target_pairs={{0,6},{1,7},{2,4},{3,5},{4,2},{5,3},{6,0},{7,1},{8,14},{9,15},{10,... | collective-permute-start | bytes 196616 | tf_op jit(solution)/shard_map/ppermute | solution.py:28
  6.2 0.0 collective-permute-start.1
  6.2 0.6 %collective-permute-start.2 = (bf16[2,64,256]{2,1,0:T(8,128)(2,1)S(1)}, bf16[2,64,256]{2,1,0:T(8,128)(2,1)S(1)}, u32[]{:S(2)}, u32[]{:S(2)}) collective-permute-start(bf16[2,64,256]{2,1,0:T(8,128)(2,1)S(1)} %get-tuple-element.29), channel_id=1, source_target_pairs={{0,2},{1,3},{2,0},{3,1},{4,6},{5,7},{6,4},{7,5},{8,10},{9,11},{10,... | collective-permute-start | bytes 196616 | tf_op jit(solution)/shard_map/ppermute | solution.py:28
  6.8 3.7 %collective-permute-start.3 = (bf16[64,256]{1,0:T(8,128)(2,1)S(1)}, bf16[64,256]{1,0:T(8,128)(2,1)S(1)}, u32[]{:S(2)}, u32[]{:S(2)}) collective-permute-start(bf16[64,256]{1,0:T(8,128)(2,1)S(1)} %get-tuple-element.33), channel_id=1, source_target_pairs={{0,6},{1,7},{2,4},{3,5},{4,2},{5,3},{6,0},{7,1},{8,14},{9,15},{10,... | collective-permute-start | bytes 98312 | tf_op jit(solution)/shard_map/ppermute | solution.py:28
  10.6 0.0 collective-permute-start.4
  10.6 0.0 collective-permute-done.refs_0_
  10.6 0.8 %collective-permute-start.5 = (bf16[64,256]{1,0:T(8,128)(2,1)S(1)}, bf16[64,256]{1,0:T(8,128)(2,1)S(1)}, u32[]{:S(2)}, u32[]{:S(2)}) collective-permute-start(bf16[64,256]{1,0:T(8,128)(2,1)S(1)} %get-tuple-element.35), channel_id=1, source_target_pairs={{0,2},{1,3},{2,0},{3,1},{4,6},{5,7},{6,4},{7,5},{8,10},{9,11},{10,... | collective-permute-start | bytes 98312 | tf_op jit(solution)/shard_map/ppermute | solution.py:28
  11.4 1.5 %collective-permute-done.1.refs_1_ = bf16[2,64,256]{2,1,0:T(8,128)(2,1)S(1)} collective-permute-done((bf16[2,64,256]{2,1,0:T(8,128)(2,1)S(1)}, bf16[2,64,256]{2,1,0:T(8,128)(2,1)S(1)}, u32[]{:S(2)}, u32[]{:S(2)}) %collective-permute-start.1) | collective-permute-done | bytes 65568 | tf_op jit(solution)/shard_map/ppermute | solution.py:28
  12.8 0.0 collective-permute-done.2.refs_2_
  12.9 1.5 %collective-permute-start.8 = (bf16[256,256]{1,0:T(8,128)(2,1)S(1)}, bf16[256,256]{1,0:T(8,128)(2,1)S(1)}, u32[]{:S(2)}, u32[]{:S(2)}) collective-permute-start(bf16[256,256]{1,0:T(8,128)(2,1)S(1)} %get-tuple-element.32.own_k.mine_ref), channel_id=1, source_target_pairs={{0,8},{8,0},{16,24},{24,16},{1,9},{9,1},{17,25},{25,17},{2,10},{10... | collective-permute-start | bytes 393224 | tf_op jit(solution)/shard_map/ppermute | solution.py:90
  14.3 0.0 collective-permute-done.3.refs_0_
  14.3 1.0 %collective-permute-done.4.refs_1_ = bf16[64,256]{1,0:T(8,128)(2,1)S(1)} collective-permute-done((bf16[64,256]{1,0:T(8,128)(2,1)S(1)}, bf16[64,256]{1,0:T(8,128)(2,1)S(1)}, u32[]{:S(2)}, u32[]{:S(2)}) %collective-permute-start.4) | collective-permute-done | bytes 32800 | tf_op jit(solution)/shard_map/ppermute | solution.py:28
  15.4 0.0 collective-permute-done.5.refs_2_
  15.4 1.6 %collective-permute-start.11 = (bf16[256,256]{1,0:T(8,128)(2,1)S(1)}, bf16[256,256]{1,0:T(8,128)(2,1)S(1)}, u32[]{:S(2)}, u32[]{:S(2)}) collective-permute-start(bf16[256,256]{1,0:T(8,128)(2,1)S(1)} %join.3.own_v.mine_ref), channel_id=1, source_target_pairs={{0,16},{8,24},{16,0},{24,8},{1,17},{9,25},{17,1},{25,9},{2,18},{10... | collective-permute-start | bytes 393224 | tf_op jit(solution)/shard_map/ppermute | solution.py:90
  17.0 0.0 collective-permute-start.6
  17.0 0.5 %collective-permute-start.7 = (bf16[256,256]{1,0:T(8,128)(2,1)S(1)}, bf16[256,256]{1,0:T(8,128)(2,1)S(1)}, u32[]{:S(2)}, u32[]{:S(2)}) collective-permute-start(bf16[256,256]{1,0:T(8,128)(2,1)S(1)} %join.3.own_v.mine_ref), channel_id=1, source_target_pairs={{0,1},{1,0},{2,3},{3,2},{4,5},{5,4},{6,7},{7,6},{8,9},{9,8},{10,11... | collective-permute-start | bytes 393224 | tf_op jit(solution)/shard_map/ppermute | solution.py:28
  18.1 0.0 collective-permute-done.8.theirs_ref
  18.2 0.0 copy-start
  18.2 1.2 %collective-permute-start.9 = (bf16[256,256]{1,0:T(8,128)(2,1)S(1)}, bf16[256,256]{1,0:T(8,128)(2,1)S(1)}, u32[]{:S(2)}, u32[]{:S(2)}) collective-permute-start(bf16[256,256]{1,0:T(8,128)(2,1)S(1)} %choose.4.mine_ref), channel_id=1, source_target_pairs={{0,16},{8,24},{16,0},{24,8},{1,17},{9,25},{17,1},{25,9},{2,18},{10... | collective-permute-start | bytes 393224 | tf_op jit(solution)/shard_map/ppermute | solution.py:90
  19.4 1.0 %collective-permute-done.11.theirs_ref = bf16[256,256]{1,0:T(8,128)(2,1)S(1)} collective-permute-done((bf16[256,256]{1,0:T(8,128)(2,1)S(1)}, bf16[256,256]{1,0:T(8,128)(2,1)S(1)}, u32[]{:S(2)}, u32[]{:S(2)}) %collective-permute-start.11) | collective-permute-done | bytes 131104 | tf_op jit(solution)/shard_map/ppermute | solution.py:90
  20.4 1.6 %collective-permute-start.12 = (bf16[256,256]{1,0:T(8,128)(2,1)S(1)}, bf16[256,256]{1,0:T(8,128)(2,1)S(1)}, u32[]{:S(2)}, u32[]{:S(2)}) collective-permute-start(bf16[256,256]{1,0:T(8,128)(2,1)S(1)} %choose.6.mine_ref), channel_id=1, source_target_pairs={{0,8},{8,0},{16,24},{24,16},{1,9},{9,1},{17,25},{25,17},{2,10},{10... | collective-permute-start | bytes 393224 | tf_op jit(solution)/shard_map/ppermute | solution.py:90
  22.0 0.0 collective-permute-done.6.other_k
  22.0 0.0 collective-permute-done.7.other_v
  22.0 0.0 copy-done
  22.0 0.9 %near.1 = (f32[2,256,128]{2,1,0:T(8,128)S(1)}, f32[2,256,128]{2,1,0:T(8,128)S(1)}, f32[256,256]{1,0:T(8,128)S(1)}, f32[8,128]{1,0:T(8,128)S(1)}) custom-call(bf16[256,256]{1,0:T(8,128)(2,1)S(1)} %get-tuple-element.31.refs_4_.q_ref, bf16[256,256]{1,0:T(8,128)(2,1)S(1)} %get-tuple-element.32.own_k.mine_ref, bf16[256,256]{1,0:T(8,128)(2,1)S(1)} %join.3.own_v.mine_ref, ...), custom_call_target="tpu_custom_call" | custom-call | flops 134217728 | tf_op jit(solution)/shard_map/near/pallas_call | solution.py:200
  23.0 0.7 %collective-permute-done.9.theirs_ref = bf16[256,256]{1,0:T(8,128)(2,1)S(1)} collective-permute-done((bf16[256,256]{1,0:T(8,128)(2,1)S(1)}, bf16[256,256]{1,0:T(8,128)(2,1)S(1)}, u32[]{:S(2)}, u32[]{:S(2)}) %collective-permute-start.9) | collective-permute-done | bytes 131104 | tf_op jit(solution)/shard_map/ppermute | solution.py:90
  23.7 0.1 collective-permute-start.10
  23.8 1.7 %collective-permute-done.12.theirs_ref = bf16[256,256]{1,0:T(8,128)(2,1)S(1)} collective-permute-done((bf16[256,256]{1,0:T(8,128)(2,1)S(1)}, bf16[256,256]{1,0:T(8,128)(2,1)S(1)}, u32[]{:S(2)}, u32[]{:S(2)}) %collective-permute-start.12) | collective-permute-done | bytes 131104 | tf_op jit(solution)/shard_map/ppermute | solution.py:90
  25.5 0.1 collective-permute-start.13
  25.6 0.0 collective-permute-done.10.other_k
  25.6 1.3 %far_weights.1 = (bf16[2,256,256]{2,1,0:T(8,128)(2,1)S(1)}, bf16[2,256,256]{2,1,0:T(8,128)(2,1)S(1)}, f32[2,256,128]{2,1,0:T(8,128)S(1)}, f32[2,256,128]{2,1,0:T(8,128)S(1)}) custom-call(s32[1]{0:T(128)S(6)} %copy.6.anchor_ref, bf16[256,256]{1,0:T(8,128)(2,1)S(1)} %get-tuple-element.31.refs_4_.q_ref, f32[2,256,128]{2,1,0:T(8,128)S(1)} %get-tuple-element.37.old_ref.refs_0_, ...), custom_call_target="tpu_custom_call" | custom-call | flops 134217728 | tf_op jit(solution)/shard_map/far_weights/pallas_call | solution.py:244
  26.8 0.1 collective-permute-done.13.refs_8_
  26.9 0.3 far_values.1
  27.2 2.2 %collective-permute-start.14 = (bf16[64,256]{1,0:T(8,128)(2,1)S(1)}, bf16[64,256]{1,0:T(8,128)(2,1)S(1)}, u32[]{:S(2)}, u32[]{:S(2)}) collective-permute-start(bf16[64,256]{1,0:T(8,128)(2,1)S(1)} %get-tuple-element.45), channel_id=1, source_target_pairs={{0,6},{1,7},{2,4},{3,5},{4,2},{5,3},{6,0},{7,1},{8,14},{9,15},{10,... | collective-permute-start | bytes 98312 | tf_op jit(solution)/shard_map/ppermute | solution.py:28
  29.4 0.0 collective-permute-start.15
  29.4 2.2 %collective-permute-start.16 = (bf16[64,256]{1,0:T(8,128)(2,1)S(1)}, bf16[64,256]{1,0:T(8,128)(2,1)S(1)}, u32[]{:S(2)}, u32[]{:S(2)}) collective-permute-start(bf16[64,256]{1,0:T(8,128)(2,1)S(1)} %get-tuple-element.47), channel_id=1, source_target_pairs={{0,2},{1,3},{2,0},{3,1},{4,6},{5,7},{6,4},{7,5},{8,10},{9,11},{10,... | collective-permute-start | bytes 98312 | tf_op jit(solution)/shard_map/ppermute | solution.py:28
  31.7 1.4 %collective-permute-done.14.refs_0_ = bf16[64,256]{1,0:T(8,128)(2,1)S(1)} collective-permute-done((bf16[64,256]{1,0:T(8,128)(2,1)S(1)}, bf16[64,256]{1,0:T(8,128)(2,1)S(1)}, u32[]{:S(2)}, u32[]{:S(2)}) %collective-permute-start.14) | collective-permute-done | bytes 32800 | tf_op jit(solution)/shard_map/ppermute | solution.py:28
  33.0 1.4 %collective-permute-done.15.refs_1_ = bf16[64,256]{1,0:T(8,128)(2,1)S(1)} collective-permute-done((bf16[64,256]{1,0:T(8,128)(2,1)S(1)}, bf16[64,256]{1,0:T(8,128)(2,1)S(1)}, u32[]{:S(2)}, u32[]{:S(2)}) %collective-permute-start.15) | collective-permute-done | bytes 32800 | tf_op jit(solution)/shard_map/ppermute | solution.py:28
  34.5 0.0 collective-permute-done.16.refs_2_
  34.5 0.7 %unpack.1 = bf16[1,64,1024]{2,1,0:T(8,128)(2,1)} custom-call(bf16[64,256]{1,0:T(8,128)(2,1)S(1)} %collective-permute-done.14.refs_0_, bf16[64,256]{1,0:T(8,128)(2,1)S(1)} %collective-permute-done.15.refs_1_, bf16[64,256]{1,0:T(8,128)(2,1)S(1)} %collective-permute-done.16.refs_2_, bf16[64,256]{1,0:T(8,128)(2,1)S(1)} %get-tuple-element.48.refs_3_), custom_call_target="tpu_custom_call" | custom-call | tf_op jit(solution)/shard_map/unpack/pallas_call | solution.py:309
  (6 shorter events, 0.1 us)
Async XLA Ops:
  1.0 9.5 %collective-permute-start = (bf16[2,64,256]{2,1,0:T(8,128)(2,1)S(1)}, bf16[2,64,256]{2,1,0:T(8,128)(2,1)S(1)}, u32[]{:S(2)}, u32[]{:S(2)}) collective-permute-start(bf16[2,64,256]{2,1,0:T(8,128)(2,1)S(1)} %get-tuple-element.27), channel_id=1, source_target_pairs={{0,6},{1,7},{2,4},{3,5},{4,2},{5,3},{6,0},{7,1},{8,14},{9,15},{10,... | collective-permute-start | bytes 196616 | tf_op jit(solution)/shard_map/ppermute | solution.py:28
  6.2 6.7 %collective-permute-start.1 = (bf16[2,64,256]{2,1,0:T(8,128)(2,1)S(1)}, bf16[2,64,256]{2,1,0:T(8,128)(2,1)S(1)}, u32[]{:S(2)}, u32[]{:S(2)}) collective-permute-start(bf16[2,64,256]{2,1,0:T(8,128)(2,1)S(1)} %get-tuple-element.28), channel_id=1, source_target_pairs={{0,4},{1,5},{2,6},{3,7},{4,0},{5,1},{6,2},{7,3},{8,12},{9,13},{10,... | collective-permute-start | bytes 196616 | tf_op jit(solution)/shard_map/ppermute | solution.py:28
  6.2 6.7 %collective-permute-start.2 = (bf16[2,64,256]{2,1,0:T(8,128)(2,1)S(1)}, bf16[2,64,256]{2,1,0:T(8,128)(2,1)S(1)}, u32[]{:S(2)}, u32[]{:S(2)}) collective-permute-start(bf16[2,64,256]{2,1,0:T(8,128)(2,1)S(1)} %get-tuple-element.29), channel_id=1, source_target_pairs={{0,2},{1,3},{2,0},{3,1},{4,6},{5,7},{6,4},{7,5},{8,10},{9,11},{10,... | collective-permute-start | bytes 196616 | tf_op jit(solution)/shard_map/ppermute | solution.py:28
  6.8 7.5 %collective-permute-start.3 = (bf16[64,256]{1,0:T(8,128)(2,1)S(1)}, bf16[64,256]{1,0:T(8,128)(2,1)S(1)}, u32[]{:S(2)}, u32[]{:S(2)}) collective-permute-start(bf16[64,256]{1,0:T(8,128)(2,1)S(1)} %get-tuple-element.33), channel_id=1, source_target_pairs={{0,6},{1,7},{2,4},{3,5},{4,2},{5,3},{6,0},{7,1},{8,14},{9,15},{10,... | collective-permute-start | bytes 98312 | tf_op jit(solution)/shard_map/ppermute | solution.py:28
  10.6 4.8 %collective-permute-start.4 = (bf16[64,256]{1,0:T(8,128)(2,1)S(1)}, bf16[64,256]{1,0:T(8,128)(2,1)S(1)}, u32[]{:S(2)}, u32[]{:S(2)}) collective-permute-start(bf16[64,256]{1,0:T(8,128)(2,1)S(1)} %get-tuple-element.34), channel_id=1, source_target_pairs={{0,4},{1,5},{2,6},{3,7},{4,0},{5,1},{6,2},{7,3},{8,12},{9,13},{10,... | collective-permute-start | bytes 98312 | tf_op jit(solution)/shard_map/ppermute | solution.py:28
  10.6 4.8 %collective-permute-start.5 = (bf16[64,256]{1,0:T(8,128)(2,1)S(1)}, bf16[64,256]{1,0:T(8,128)(2,1)S(1)}, u32[]{:S(2)}, u32[]{:S(2)}) collective-permute-start(bf16[64,256]{1,0:T(8,128)(2,1)S(1)} %get-tuple-element.35), channel_id=1, source_target_pairs={{0,2},{1,3},{2,0},{3,1},{4,6},{5,7},{6,4},{7,5},{8,10},{9,11},{10,... | collective-permute-start | bytes 98312 | tf_op jit(solution)/shard_map/ppermute | solution.py:28
  12.9 5.3 %collective-permute-start.8 = (bf16[256,256]{1,0:T(8,128)(2,1)S(1)}, bf16[256,256]{1,0:T(8,128)(2,1)S(1)}, u32[]{:S(2)}, u32[]{:S(2)}) collective-permute-start(bf16[256,256]{1,0:T(8,128)(2,1)S(1)} %get-tuple-element.32.own_k.mine_ref), channel_id=1, source_target_pairs={{0,8},{8,0},{16,24},{24,16},{1,9},{9,1},{17,25},{25,17},{2,10},{10... | collective-permute-start | bytes 393224 | tf_op jit(solution)/shard_map/ppermute | solution.py:90
  15.4 5.0 %collective-permute-start.11 = (bf16[256,256]{1,0:T(8,128)(2,1)S(1)}, bf16[256,256]{1,0:T(8,128)(2,1)S(1)}, u32[]{:S(2)}, u32[]{:S(2)}) collective-permute-start(bf16[256,256]{1,0:T(8,128)(2,1)S(1)} %join.3.own_v.mine_ref), channel_id=1, source_target_pairs={{0,16},{8,24},{16,0},{24,8},{1,17},{9,25},{17,1},{25,9},{2,18},{10... | collective-permute-start | bytes 393224 | tf_op jit(solution)/shard_map/ppermute | solution.py:90
  17.0 5.0 %collective-permute-start.6 = (bf16[256,256]{1,0:T(8,128)(2,1)S(1)}, bf16[256,256]{1,0:T(8,128)(2,1)S(1)}, u32[]{:S(2)}, u32[]{:S(2)}) collective-permute-start(bf16[256,256]{1,0:T(8,128)(2,1)S(1)} %get-tuple-element.32.own_k.mine_ref), channel_id=1, source_target_pairs={{0,1},{1,0},{2,3},{3,2},{4,5},{5,4},{6,7},{7,6},{8,9},{9,8},{10,11... | collective-permute-start | bytes 393224 | tf_op jit(solution)/shard_map/ppermute | solution.py:28
  17.0 5.0 %collective-permute-start.7 = (bf16[256,256]{1,0:T(8,128)(2,1)S(1)}, bf16[256,256]{1,0:T(8,128)(2,1)S(1)}, u32[]{:S(2)}, u32[]{:S(2)}) collective-permute-start(bf16[256,256]{1,0:T(8,128)(2,1)S(1)} %join.3.own_v.mine_ref), channel_id=1, source_target_pairs={{0,1},{1,0},{2,3},{3,2},{4,5},{5,4},{6,7},{7,6},{8,9},{9,8},{10,11... | collective-permute-start | bytes 393224 | tf_op jit(solution)/shard_map/ppermute | solution.py:28
  18.2 3.8 %copy-start = (s32[1,512]{1,0:T(1,128)S(1)}, s32[1,512]{1,0:T(1,128)}, u32[]{:S(2)}) copy-start(s32[1,512]{1,0:T(1,128)} %at.1) | copy-start | bytes 6148
  18.2 5.5 %collective-permute-start.9 = (bf16[256,256]{1,0:T(8,128)(2,1)S(1)}, bf16[256,256]{1,0:T(8,128)(2,1)S(1)}, u32[]{:S(2)}, u32[]{:S(2)}) collective-permute-start(bf16[256,256]{1,0:T(8,128)(2,1)S(1)} %choose.4.mine_ref), channel_id=1, source_target_pairs={{0,16},{8,24},{16,0},{24,8},{1,17},{9,25},{17,1},{25,9},{2,18},{10... | collective-permute-start | bytes 393224 | tf_op jit(solution)/shard_map/ppermute | solution.py:90
  20.4 5.0 %collective-permute-start.12 = (bf16[256,256]{1,0:T(8,128)(2,1)S(1)}, bf16[256,256]{1,0:T(8,128)(2,1)S(1)}, u32[]{:S(2)}, u32[]{:S(2)}) collective-permute-start(bf16[256,256]{1,0:T(8,128)(2,1)S(1)} %choose.6.mine_ref), channel_id=1, source_target_pairs={{0,8},{8,0},{16,24},{24,16},{1,9},{9,1},{17,25},{25,17},{2,10},{10... | collective-permute-start | bytes 393224 | tf_op jit(solution)/shard_map/ppermute | solution.py:90
  23.7 1.9 %collective-permute-start.10 = (bf16[256,256]{1,0:T(8,128)(2,1)S(1)}, bf16[256,256]{1,0:T(8,128)(2,1)S(1)}, u32[]{:S(2)}, u32[]{:S(2)}) collective-permute-start(bf16[256,256]{1,0:T(8,128)(2,1)S(1)} %choose.5.own_k), channel_id=1, source_target_pairs={{0,1},{1,0},{2,3},{3,2},{4,5},{5,4},{6,7},{7,6},{8,9},{9,8},{10,11... | collective-permute-start | bytes 393224 | tf_op jit(solution)/shard_map/ppermute | solution.py:28
  25.5 1.4 %collective-permute-start.13 = (bf16[256,256]{1,0:T(8,128)(2,1)S(1)}, bf16[256,256]{1,0:T(8,128)(2,1)S(1)}, u32[]{:S(2)}, u32[]{:S(2)}) collective-permute-start(bf16[256,256]{1,0:T(8,128)(2,1)S(1)} %choose.7.refs_7_), channel_id=1, source_target_pairs={{0,1},{1,0},{2,3},{3,2},{4,5},{5,4},{6,7},{7,6},{8,9},{9,8},{10,11... | collective-permute-start | bytes 393224 | tf_op jit(solution)/shard_map/ppermute | solution.py:28
  27.2 5.8 %collective-permute-start.14 = (bf16[64,256]{1,0:T(8,128)(2,1)S(1)}, bf16[64,256]{1,0:T(8,128)(2,1)S(1)}, u32[]{:S(2)}, u32[]{:S(2)}) collective-permute-start(bf16[64,256]{1,0:T(8,128)(2,1)S(1)} %get-tuple-element.45), channel_id=1, source_target_pairs={{0,6},{1,7},{2,4},{3,5},{4,2},{5,3},{6,0},{7,1},{8,14},{9,15},{10,... | collective-permute-start | bytes 98312 | tf_op jit(solution)/shard_map/ppermute | solution.py:28
  29.4 5.0 %collective-permute-start.15 = (bf16[64,256]{1,0:T(8,128)(2,1)S(1)}, bf16[64,256]{1,0:T(8,128)(2,1)S(1)}, u32[]{:S(2)}, u32[]{:S(2)}) collective-permute-start(bf16[64,256]{1,0:T(8,128)(2,1)S(1)} %get-tuple-element.46), channel_id=1, source_target_pairs={{0,4},{1,5},{2,6},{3,7},{4,0},{5,1},{6,2},{7,3},{8,12},{9,13},{10,... | collective-permute-start | bytes 98312 | tf_op jit(solution)/shard_map/ppermute | solution.py:28
  29.4 5.0 %collective-permute-start.16 = (bf16[64,256]{1,0:T(8,128)(2,1)S(1)}, bf16[64,256]{1,0:T(8,128)(2,1)S(1)}, u32[]{:S(2)}, u32[]{:S(2)}) collective-permute-start(bf16[64,256]{1,0:T(8,128)(2,1)S(1)} %get-tuple-element.47), channel_id=1, source_target_pairs={{0,2},{1,3},{2,0},{3,1},{4,6},{5,7},{6,4},{7,5},{8,10},{9,11},{10,... | collective-permute-start | bytes 98312 | tf_op jit(solution)/shard_map/ppermute | solution.py:28

commit v3 on v2

--- a/solution.py
+++ b/solution.py
@@ -12,6 +12,7 @@
 NEG = -1e30
 EXP_SCALE = 1.0 / (math.sqrt(HD) * math.log(2.0))
 VMEM_LIMIT = 48 * 2**20
+QUERY_FLOPS = 10**10
 ANY = pl.BlockSpec(memory_space=pl.ANY)
 SMEM = pl.BlockSpec(memory_space=pltpu.SMEM)
 
@@ -33,13 +34,13 @@
     rows, width = queries.shape[1], queries.shape[2] // chips
 
     def body(q_ref, k_ref, v_ref, *rest):
-        qk_refs, v_refs, sems = rest[:chips], rest[chips : 2 * chips], rest[-1]
+        kv_refs, q_refs, sems = rest[:chips], rest[chips : 2 * chips], rest[-1]
         chip = lax.axis_index("sp") // CORES
         copies = []
         for flip in reversed(range(chips)):
             columns = pl.ds(pl.multiple_of((chip ^ flip) * width, HD), width)
-            targets = (qk_refs[flip].at[0], qk_refs[flip].at[1], v_refs[flip])
-            for part, source in enumerate((q_ref, k_ref, v_ref)):
+            targets = (kv_refs[flip].at[0], kv_refs[flip].at[1], q_refs[flip])
+            for part, source in enumerate((k_ref, v_ref, q_ref)):
                 copies.append(
                     pltpu.make_async_copy(
                         source.at[0, :, columns], targets[part], sems.at[3 * flip + part]
@@ -62,23 +63,38 @@
     return outs[:chips], outs[chips:]
 
 
-def join(blocks, order, after=()):
+def join(blocks, order, flops=0):
     chips, parts = len(blocks), blocks[0].shape[:-2]
     rows, width = blocks[0].shape[-2:]
     count = parts[0] if parts else 1
 
     def body(*refs):
         for flip, block in zip((*order, 0), refs[:chips]):
-            for part, out in enumerate(refs[chips + len(after) :]):
+            for part, out in enumerate(refs[chips:]):
                 out[chip_rows(flip, rows), :] = block[part] if parts else block[...]
 
     return pl.pallas_call(
         body,
         out_shape=[pltpu.VMEM((chips * rows, width), blocks[0].dtype)] * count,
-        in_specs=in_vmem(chips + len(after)),
+        in_specs=in_vmem(chips),
         out_specs=in_vmem(count),
+        cost_estimate=pl.CostEstimate(flops=flops, bytes_accessed=0, transcendentals=0),
         name="join",
-    )(*resident(*[blocks[flip] for flip in (*order, 0)], *after))
+    )(*resident(*[blocks[flip] for flip in (*order, 0)]))
+
+
+def pair(first, second):
+    def body(first_ref, second_ref, out_ref):
+        out_ref[0] = first_ref[...]
+        out_ref[1] = second_ref[...]
+
+    return pl.pallas_call(
+        body,
+        out_shape=pltpu.VMEM((2, *first.shape), first.dtype),
+        in_specs=in_vmem(2),
+        out_specs=in_vmem(1)[0],
+        name="pair",
+    )(*resident(first, second))
 
 
 def chip_rows(flip, rows):
@@ -150,7 +166,7 @@
     return first.astype(jnp.bfloat16), second.astype(jnp.bfloat16), top, total
 
 
-def near(q_rows, own, other, positions):
+def near(q_rows, own_k, own_v, other, positions):
     length, width = q_rows.shape
     chips = lax.axis_size("sp") // CORES
     rows = length // chips
@@ -170,8 +186,9 @@
             jnp.concatenate([jnp.where(low, turned[c], tokens[c + 1]) for c in pairs], 1),
         ]
 
-    def body(q_ref, own_k, own_v, other_k, other_v, at, top_ref, sum_ref, acc_ref, end_ref, own_at):
+    def body(q_ref, own_k, own_v, other_kv, at, top_ref, sum_ref, acc_ref, end_ref, own_at):
         end_ref[...] = jnp.zeros_like(end_ref)
+        other_k, other_v = other_kv.at[0], other_kv.at[1]
         core = lax.axis_index("sp") % CORES
         first_at, second_at = split(at)
         own_at[...] = jnp.where(core == 0, first_at, second_at)
@@ -205,13 +222,13 @@
             pltpu.VMEM((length, width), jnp.float32),
             pltpu.VMEM((8, HD), jnp.float32),
         ],
-        in_specs=in_vmem(6),
+        in_specs=in_vmem(5),
         out_specs=in_vmem(4),
         scratch_shapes=[pltpu.VMEM((8, length), jnp.int32)],
         compiler_params=pltpu.CompilerParams(vmem_limit_bytes=VMEM_LIMIT),
         cost_estimate=cost(length, width),
         name="near",
-    )(*resident(q_rows, *own, *other), positions)
+    )(*resident(q_rows, own_k, own_v, other), positions)
 
 
 def far_weights(q_rows, top, own_k, other_k, anchor):
@@ -322,24 +339,25 @@
 
 
 def on_device(queries, keys, values, positions, anchor):
-    order = tuple(reversed(range(1, lax.axis_size("sp") // CORES)))
-    qk_blocks, v_blocks = pack(queries, keys, values)
-    q_rows, k_own = join(trade(qk_blocks, order), order)
-    (v_own,) = join(trade(v_blocks, order), order, [q_rows])
-    own = k_own, v_own
-    other = [swap(x, 1) for x in own]
-    *state, end = near(q_rows, own, other, positions)
+    chips = lax.axis_size("sp") // CORES
+    distant_first = tuple(reversed(range(1, chips)))
+    crossing_first = tuple(sorted(range(1, chips), key=lambda flip: (flip < chips // 2, flip)))
+
+    kv_blocks, q_blocks = pack(queries, keys, values)
+    k_own, v_own = join(trade(kv_blocks, crossing_first), crossing_first)
+    (q_rows,) = join(trade(q_blocks, distant_first), distant_first, QUERY_FLOPS)
+    other = swap(pair(k_own, v_own), 1)
 
     bits = lax.axis_size("grp").bit_length() - 1
-    k_far, v_far = own
+    k_far, v_far, *state, end = k_own, v_own, *near(q_rows, k_own, v_own, other, positions)
     for stage in range(bits):
-        after = [end] if stage == 1 else ()
+        after = [[q_rows], [end]][stage] if stage < 2 else ()
+        back = bits - 1 - stage
         k_far = choose(k_far, turn(k_far, stage), anchor, stage, after)
-        back = bits - 1 - stage
         v_far = choose(v_far, turn(v_far, back), anchor, back)
     far_state = far_weights(q_rows, state[0], k_far, swap(k_far, 1), anchor)
     done = far_values(state, far_state, v_far, swap(v_far, 1))
-    return unpack(trade(done, order), order)
+    return unpack(trade(done, distant_first), distant_first)
 
 
 def solution(mesh):

time: 35.3 us -> 34.9 us (0.989)
  waiting for transfers between devices: 8.79 us -> 8.4 us
    ppermute x13 -> x12, waiting for transfers between devices: 5.37 us -> 3.76 us  [swap(): lax.ppermute(x, 'sp', [(i, i ^ flip) for i in range(lax.axis_size('sp'))])]
    ppermute x4, waiting for transfers between devices: 3.42 us -> 4.64 us  [turn(): lax.ppermute(x, 'grp', [(i, i ^ 1 << bit) for i in range(lax.axis_size('g...]
    ppermute x13 -> x12, starting transfers between devices: 15.4 us -> 15.1 us  [swap(): lax.ppermute(x, 'sp', [(i, i ^ flip) for i in range(lax.axis_size('sp'))])]
  transfers between devices with their start and end apart: 17 -> 16, of which waited for: 8 -> 7; matrix products, arithmetic and copies ran while one was open for 0% -> 0% of each run, Pallas kernels for 7% -> 7%
where the time goes in v3:
time: 34.9 us; the launch traced here: 34.7 us
  starting transfers between devices  21.2 us (61%)
  waiting for transfers between devices  8.4 us (24%)
  Pallas kernels  4.32 us (12%)
  between operations  0.79 us (2%)
    ppermute x12, starting transfers between devices, swap(): lax.ppermute(x, 'sp', [(i, i ^ flip) for i in range(lax.axis_size('sp'))])  15.1 us
    ppermute x4, starting transfers between devices, turn(): lax.ppermute(x, 'grp', [(i, i ^ 1 << bit) for i in range(lax.axis_size('g...  6.09 us
    ppermute x4, waiting for transfers between devices, turn(): lax.ppermute(x, 'grp', [(i, i ^ 1 << bit) for i in range(lax.axis_size('g...  4.64 us
    ppermute x12, waiting for transfers between devices, swap(): lax.ppermute(x, 'sp', [(i, i ^ flip) for i in range(lax.axis_size('sp'))])  3.76 us
    pallas_call x1, Pallas kernels, far_weights(): pl.pallas_call(body, out_shape=[weights, weights, state, state], in_specs...  1.26 us
    pallas_call x1, Pallas kernels, pack(): pl.pallas_call(body, out_shape=[pltpu.VMEM((2, rows, width), keys.dtype)]...  1.04 us
    pallas_call x1, Pallas kernels, near(): pl.pallas_call(body, out_shape=[state, state, pltpu.VMEM((length, width),...  0.92 us
  transfers between devices with their start and end apart: 16, of which 7 were waited for; matrix products, arithmetic and copies ran while one was open for 0% of the time, Pallas kernels for 7%

profile of v3, /device:TPU:0, one launch (start us, length us, event | category | flops | bytes accessed | tf_op | source)
XLA Modules:
  0.0 34.7 jit_solution(10203893534640397553)
XLA Ops:
  0.0 1.0 %pack.1 = (bf16[2,64,256]{2,1,0:T(8,128)(2,1)S(1)}, bf16[2,64,256]{2,1,0:T(8,128)(2,1)S(1)}, bf16[2,64,256]{2,1,0:T(8,128)(2,1)S(1)}, bf16[2,64,256]{2,1,0:T(8,1...) custom-call(bf16[1,64,1024]{2,1,0:T(8,128)(2,1)} %q_ref.1, ...), custom_call_target="tpu_custom_call" | custom-call | tf_op jit(solution)/shard_map/pack/pallas_call | solution.py:54
  1.0 4.1 %collective-permute-start.3 = (bf16[2,64,256]{2,1,0:T(8,128)(2,1)S(1)}, bf16[2,64,256]{2,1,0:T(8,128)(2,1)S(1)}, u32[]{:S(2)}, u32[]{:S(2)}) collective-permute-start(bf16[2,64,256]{2,1,0:T(8,128)(2,1)S(1)} %get-tuple-element.31), channel_id=1, source_target_pairs={{0,4},{1,5},{2,6},{3,7},{4,0},{5,1},{6,2},{7,3},{8,12},{9,13},{10,... | collective-permute-start | bytes 196616 | tf_op jit(solution)/shard_map/ppermute | solution.py:29
  5.1 1.3 %collective-permute-start.4 = (bf16[2,64,256]{2,1,0:T(8,128)(2,1)S(1)}, bf16[2,64,256]{2,1,0:T(8,128)(2,1)S(1)}, u32[]{:S(2)}, u32[]{:S(2)}) collective-permute-start(bf16[2,64,256]{2,1,0:T(8,128)(2,1)S(1)} %get-tuple-element.32), channel_id=1, source_target_pairs={{0,6},{1,7},{2,4},{3,5},{4,2},{5,3},{6,0},{7,1},{8,14},{9,15},{10,... | collective-permute-start | bytes 196616 | tf_op jit(solution)/shard_map/ppermute | solution.py:29
  6.5 0.2 collective-permute-start.5
  6.7 2.9 %collective-permute-start = (bf16[64,256]{1,0:T(8,128)(2,1)S(1)}, bf16[64,256]{1,0:T(8,128)(2,1)S(1)}, u32[]{:S(2)}, u32[]{:S(2)}) collective-permute-start(bf16[64,256]{1,0:T(8,128)(2,1)S(1)} %get-tuple-element.27), channel_id=1, source_target_pairs={{0,6},{1,7},{2,4},{3,5},{4,2},{5,3},{6,0},{7,1},{8,14},{9,15},{10,... | collective-permute-start | bytes 98312 | tf_op jit(solution)/shard_map/ppermute | solution.py:29
  9.7 0.3 collective-permute-start.1
  10.0 0.0 collective-permute-done.3.refs_0_
  10.0 1.5 %collective-permute-start.2 = (bf16[64,256]{1,0:T(8,128)(2,1)S(1)}, bf16[64,256]{1,0:T(8,128)(2,1)S(1)}, u32[]{:S(2)}, u32[]{:S(2)}) collective-permute-start(bf16[64,256]{1,0:T(8,128)(2,1)S(1)} %get-tuple-element.29), channel_id=1, source_target_pairs={{0,2},{1,3},{2,0},{3,1},{4,6},{5,7},{6,4},{7,5},{8,10},{9,11},{10,... | collective-permute-start | bytes 98312 | tf_op jit(solution)/shard_map/ppermute | solution.py:29
  12.2 0.0 collective-permute-done.4.refs_1_
  12.2 0.0 collective-permute-done.5.refs_2_
  12.2 1.6 %collective-permute-start.7 = (bf16[256,256]{1,0:T(8,128)(2,1)S(1)}, bf16[256,256]{1,0:T(8,128)(2,1)S(1)}, u32[]{:S(2)}, u32[]{:S(2)}) collective-permute-start(bf16[256,256]{1,0:T(8,128)(2,1)S(1)} %get-tuple-element.35.first_ref.own_k.mine_ref), channel_id=1, source_target_pairs={{0,8},{8,0},{16,24},{24,16},{1,9},{9,1},{17,25},{25,17},{2,10},{10... | collective-permute-start | bytes 393224 | tf_op jit(solution)/shard_map/ppermute | solution.py:106
  13.8 1.6 %collective-permute-start.10 = (bf16[256,256]{1,0:T(8,128)(2,1)S(1)}, bf16[256,256]{1,0:T(8,128)(2,1)S(1)}, u32[]{:S(2)}, u32[]{:S(2)}) collective-permute-start(bf16[256,256]{1,0:T(8,128)(2,1)S(1)} %get-tuple-element.36.second_ref.own_v.mine_ref), channel_id=1, source_target_pairs={{0,16},{8,24},{16,0},{24,8},{1,17},{9,25},{17,1},{25,9},{2,18},{10... | collective-permute-start | bytes 393224 | tf_op jit(solution)/shard_map/ppermute | solution.py:106
  15.4 0.0 collective-permute-done.refs_0_
  15.4 0.0 collective-permute-start.6
  15.4 0.0 collective-permute-done.1.refs_1_
  15.4 0.0 collective-permute-done.2.refs_2_
  15.5 1.8 %collective-permute-done.7.theirs_ref = bf16[256,256]{1,0:T(8,128)(2,1)S(1)} collective-permute-done((bf16[256,256]{1,0:T(8,128)(2,1)S(1)}, bf16[256,256]{1,0:T(8,128)(2,1)S(1)}, u32[]{:S(2)}, u32[]{:S(2)}) %collective-permute-start.7) | collective-permute-done | bytes 131104 | tf_op jit(solution)/shard_map/ppermute | solution.py:106
  17.3 0.0 copy-start
  17.3 1.6 %collective-permute-start.8 = (bf16[256,256]{1,0:T(8,128)(2,1)S(1)}, bf16[256,256]{1,0:T(8,128)(2,1)S(1)}, u32[]{:S(2)}, u32[]{:S(2)}) collective-permute-start(bf16[256,256]{1,0:T(8,128)(2,1)S(1)} %choose.4.mine_ref), channel_id=1, source_target_pairs={{0,16},{8,24},{16,0},{24,8},{1,17},{9,25},{17,1},{25,9},{2,18},{10... | collective-permute-start | bytes 393224 | tf_op jit(solution)/shard_map/ppermute | solution.py:106
  18.9 0.2 collective-permute-done.10.theirs_ref
  19.1 1.4 %collective-permute-start.11 = (bf16[256,256]{1,0:T(8,128)(2,1)S(1)}, bf16[256,256]{1,0:T(8,128)(2,1)S(1)}, u32[]{:S(2)}, u32[]{:S(2)}) collective-permute-start(bf16[256,256]{1,0:T(8,128)(2,1)S(1)} %choose.6.mine_ref), channel_id=1, source_target_pairs={{0,8},{8,0},{16,24},{24,16},{1,9},{9,1},{17,25},{25,17},{2,10},{10... | collective-permute-start | bytes 393224 | tf_op jit(solution)/shard_map/ppermute | solution.py:106
  20.5 0.0 collective-permute-done.6.other_kv
  20.5 0.0 copy-done
  20.5 0.9 %near.1 = (f32[2,256,128]{2,1,0:T(8,128)S(1)}, f32[2,256,128]{2,1,0:T(8,128)S(1)}, f32[256,256]{1,0:T(8,128)S(1)}, f32[8,128]{1,0:T(8,128)S(1)}) custom-call(bf16[256,256]{1,0:T(8,128)(2,1)S(1)} %join.2.q_ref.rest_0_, bf16[256,256]{1,0:T(8,128)(2,1)S(1)} %get-tuple-element.35.first_ref.own_k.mine_ref, ...), custom_call_target="tpu_custom_call" | custom-call | flops 134217728 | tf_op jit(solution)/shard_map/near/pallas_call | solution.py:217
  21.4 0.9 %collective-permute-done.8.theirs_ref = bf16[256,256]{1,0:T(8,128)(2,1)S(1)} collective-permute-done((bf16[256,256]{1,0:T(8,128)(2,1)S(1)}, bf16[256,256]{1,0:T(8,128)(2,1)S(1)}, u32[]{:S(2)}, u32[]{:S(2)}) %collective-permute-start.8) | collective-permute-done | bytes 131104 | tf_op jit(solution)/shard_map/ppermute | solution.py:106
  22.3 0.1 collective-permute-start.9
  22.4 1.7 %collective-permute-done.11.theirs_ref = bf16[256,256]{1,0:T(8,128)(2,1)S(1)} collective-permute-done((bf16[256,256]{1,0:T(8,128)(2,1)S(1)}, bf16[256,256]{1,0:T(8,128)(2,1)S(1)}, u32[]{:S(2)}, u32[]{:S(2)}) %collective-permute-start.11) | collective-permute-done | bytes 131104 | tf_op jit(solution)/shard_map/ppermute | solution.py:106
  24.1 0.1 collective-permute-start.12
  24.2 0.0 collective-permute-done.9.other_k
  24.2 1.3 %far_weights.1 = (bf16[2,256,256]{2,1,0:T(8,128)(2,1)S(1)}, bf16[2,256,256]{2,1,0:T(8,128)(2,1)S(1)}, f32[2,256,128]{2,1,0:T(8,128)S(1)}, f32[2,256,128]{2,1,0:T(8,128)S(1)}) custom-call(s32[1]{0:T(128)S(6)} %copy.6.anchor_ref, bf16[256,256]{1,0:T(8,128)(2,1)S(1)} %join.2.q_ref.rest_0_, f32[2,256,128]{2,1,0:T(8,128)S(1)} %get-tuple-element.37.old_ref.refs_0_, ...), custom_call_target="tpu_custom_call" | custom-call | flops 134217728 | tf_op jit(solution)/shard_map/far_weights/pallas_call | solution.py:261
  25.5 0.1 collective-permute-done.12.refs_8_
  25.6 0.3 far_values.1
  25.9 3.3 %collective-permute-start.13 = (bf16[64,256]{1,0:T(8,128)(2,1)S(1)}, bf16[64,256]{1,0:T(8,128)(2,1)S(1)}, u32[]{:S(2)}, u32[]{:S(2)}) collective-permute-start(bf16[64,256]{1,0:T(8,128)(2,1)S(1)} %get-tuple-element.45), channel_id=1, source_target_pairs={{0,6},{1,7},{2,4},{3,5},{4,2},{5,3},{6,0},{7,1},{8,14},{9,15},{10,... | collective-permute-start | bytes 98312 | tf_op jit(solution)/shard_map/ppermute | solution.py:29
  29.1 0.6 %collective-permute-start.14 = (bf16[64,256]{1,0:T(8,128)(2,1)S(1)}, bf16[64,256]{1,0:T(8,128)(2,1)S(1)}, u32[]{:S(2)}, u32[]{:S(2)}) collective-permute-start(bf16[64,256]{1,0:T(8,128)(2,1)S(1)} %get-tuple-element.46), channel_id=1, source_target_pairs={{0,4},{1,5},{2,6},{3,7},{4,0},{5,1},{6,2},{7,3},{8,12},{9,13},{10,... | collective-permute-start | bytes 98312 | tf_op jit(solution)/shard_map/ppermute | solution.py:29
  29.7 0.6 %collective-permute-start.15 = (bf16[64,256]{1,0:T(8,128)(2,1)S(1)}, bf16[64,256]{1,0:T(8,128)(2,1)S(1)}, u32[]{:S(2)}, u32[]{:S(2)}) collective-permute-start(bf16[64,256]{1,0:T(8,128)(2,1)S(1)} %get-tuple-element.47), channel_id=1, source_target_pairs={{0,2},{1,3},{2,0},{3,1},{4,6},{5,7},{6,4},{7,5},{8,10},{9,11},{10,... | collective-permute-start | bytes 98312 | tf_op jit(solution)/shard_map/ppermute | solution.py:29
  30.3 1.4 %collective-permute-done.13.refs_0_ = bf16[64,256]{1,0:T(8,128)(2,1)S(1)} collective-permute-done((bf16[64,256]{1,0:T(8,128)(2,1)S(1)}, bf16[64,256]{1,0:T(8,128)(2,1)S(1)}, u32[]{:S(2)}, u32[]{:S(2)}) %collective-permute-start.13) | collective-permute-done | bytes 32800 | tf_op jit(solution)/shard_map/ppermute | solution.py:29
  31.7 2.3 %collective-permute-done.14.refs_1_ = bf16[64,256]{1,0:T(8,128)(2,1)S(1)} collective-permute-done((bf16[64,256]{1,0:T(8,128)(2,1)S(1)}, bf16[64,256]{1,0:T(8,128)(2,1)S(1)}, u32[]{:S(2)}, u32[]{:S(2)}) %collective-permute-start.14) | collective-permute-done | bytes 32800 | tf_op jit(solution)/shard_map/ppermute | solution.py:29
  34.0 0.0 collective-permute-done.15.refs_2_
  34.0 0.7 %unpack.1 = bf16[1,64,1024]{2,1,0:T(8,128)(2,1)} custom-call(bf16[64,256]{1,0:T(8,128)(2,1)S(1)} %collective-permute-done.13.refs_0_, bf16[64,256]{1,0:T(8,128)(2,1)S(1)} %collective-permute-done.14.refs_1_, bf16[64,256]{1,0:T(8,128)(2,1)S(1)} %collective-permute-done.15.refs_2_, bf16[64,256]{1,0:T(8,128)(2,1)S(1)} %get-tuple-element.48.refs_3_), custom_call_target="tpu_custom_call" | custom-call | tf_op jit(solution)/shard_map/unpack/pallas_call | solution.py:326
  (7 shorter events, 0.1 us)
Async XLA Ops:
  1.0 8.9 %collective-permute-start.3 = (bf16[2,64,256]{2,1,0:T(8,128)(2,1)S(1)}, bf16[2,64,256]{2,1,0:T(8,128)(2,1)S(1)}, u32[]{:S(2)}, u32[]{:S(2)}) collective-permute-start(bf16[2,64,256]{2,1,0:T(8,128)(2,1)S(1)} %get-tuple-element.31), channel_id=1, source_target_pairs={{0,4},{1,5},{2,6},{3,7},{4,0},{5,1},{6,2},{7,3},{8,12},{9,13},{10,... | collective-permute-start | bytes 196616 | tf_op jit(solution)/shard_map/ppermute | solution.py:29
  5.1 7.0 %collective-permute-start.4 = (bf16[2,64,256]{2,1,0:T(8,128)(2,1)S(1)}, bf16[2,64,256]{2,1,0:T(8,128)(2,1)S(1)}, u32[]{:S(2)}, u32[]{:S(2)}) collective-permute-start(bf16[2,64,256]{2,1,0:T(8,128)(2,1)S(1)} %get-tuple-element.32), channel_id=1, source_target_pairs={{0,6},{1,7},{2,4},{3,5},{4,2},{5,3},{6,0},{7,1},{8,14},{9,15},{10,... | collective-permute-start | bytes 196616 | tf_op jit(solution)/shard_map/ppermute | solution.py:29
  6.5 5.7 %collective-permute-start.5 = (bf16[2,64,256]{2,1,0:T(8,128)(2,1)S(1)}, bf16[2,64,256]{2,1,0:T(8,128)(2,1)S(1)}, u32[]{:S(2)}, u32[]{:S(2)}) collective-permute-start(bf16[2,64,256]{2,1,0:T(8,128)(2,1)S(1)} %get-tuple-element.33), channel_id=1, source_target_pairs={{0,2},{1,3},{2,0},{3,1},{4,6},{5,7},{6,4},{7,5},{8,10},{9,11},{10,... | collective-permute-start | bytes 196616 | tf_op jit(solution)/shard_map/ppermute | solution.py:29
  6.7 8.7 %collective-permute-start = (bf16[64,256]{1,0:T(8,128)(2,1)S(1)}, bf16[64,256]{1,0:T(8,128)(2,1)S(1)}, u32[]{:S(2)}, u32[]{:S(2)}) collective-permute-start(bf16[64,256]{1,0:T(8,128)(2,1)S(1)} %get-tuple-element.27), channel_id=1, source_target_pairs={{0,6},{1,7},{2,4},{3,5},{4,2},{5,3},{6,0},{7,1},{8,14},{9,15},{10,... | collective-permute-start | bytes 98312 | tf_op jit(solution)/shard_map/ppermute | solution.py:29
  9.7 5.8 %collective-permute-start.1 = (bf16[64,256]{1,0:T(8,128)(2,1)S(1)}, bf16[64,256]{1,0:T(8,128)(2,1)S(1)}, u32[]{:S(2)}, u32[]{:S(2)}) collective-permute-start(bf16[64,256]{1,0:T(8,128)(2,1)S(1)} %get-tuple-element.28), channel_id=1, source_target_pairs={{0,4},{1,5},{2,6},{3,7},{4,0},{5,1},{6,2},{7,3},{8,12},{9,13},{10,... | collective-permute-start | bytes 98312 | tf_op jit(solution)/shard_map/ppermute | solution.py:29
  10.0 5.4 %collective-permute-start.2 = (bf16[64,256]{1,0:T(8,128)(2,1)S(1)}, bf16[64,256]{1,0:T(8,128)(2,1)S(1)}, u32[]{:S(2)}, u32[]{:S(2)}) collective-permute-start(bf16[64,256]{1,0:T(8,128)(2,1)S(1)} %get-tuple-element.29), channel_id=1, source_target_pairs={{0,2},{1,3},{2,0},{3,1},{4,6},{5,7},{6,4},{7,5},{8,10},{9,11},{10,... | collective-permute-start | bytes 98312 | tf_op jit(solution)/shard_map/ppermute | solution.py:29
  12.2 5.0 %collective-permute-start.7 = (bf16[256,256]{1,0:T(8,128)(2,1)S(1)}, bf16[256,256]{1,0:T(8,128)(2,1)S(1)}, u32[]{:S(2)}, u32[]{:S(2)}) collective-permute-start(bf16[256,256]{1,0:T(8,128)(2,1)S(1)} %get-tuple-element.35.first_ref.own_k.mine_ref), channel_id=1, source_target_pairs={{0,8},{8,0},{16,24},{24,16},{1,9},{9,1},{17,25},{25,17},{2,10},{10... | collective-permute-start | bytes 393224 | tf_op jit(solution)/shard_map/ppermute | solution.py:106
  13.8 5.3 %collective-permute-start.10 = (bf16[256,256]{1,0:T(8,128)(2,1)S(1)}, bf16[256,256]{1,0:T(8,128)(2,1)S(1)}, u32[]{:S(2)}, u32[]{:S(2)}) collective-permute-start(bf16[256,256]{1,0:T(8,128)(2,1)S(1)} %get-tuple-element.36.second_ref.own_v.mine_ref), channel_id=1, source_target_pairs={{0,16},{8,24},{16,0},{24,8},{1,17},{9,25},{17,1},{25,9},{2,18},{10... | collective-permute-start | bytes 393224 | tf_op jit(solution)/shard_map/ppermute | solution.py:106
  15.4 5.1 %collective-permute-start.6 = (bf16[2,256,256]{2,1,0:T(8,128)(2,1)S(1)}, bf16[2,256,256]{2,1,0:T(8,128)(2,1)S(1)}, u32[]{:S(2)}, u32[]{:S(2)}) collective-permute-start(bf16[2,256,256]{2,1,0:T(8,128)(2,1)S(1)} %pair.1), channel_id=1, source_target_pairs={{0,1},{1,0},{2,3},{3,2},{4,5},{5,4},{6,7},{7,6},{8,9},{9,8},{10,11... | collective-permute-start | bytes 786440 | tf_op jit(solution)/shard_map/ppermute | solution.py:29
  17.3 3.2 %copy-start = (s32[1,512]{1,0:T(1,128)S(1)}, s32[1,512]{1,0:T(1,128)}, u32[]{:S(2)}) copy-start(s32[1,512]{1,0:T(1,128)} %at.1) | copy-start | bytes 6148
  17.3 5.0 %collective-permute-start.8 = (bf16[256,256]{1,0:T(8,128)(2,1)S(1)}, bf16[256,256]{1,0:T(8,128)(2,1)S(1)}, u32[]{:S(2)}, u32[]{:S(2)}) collective-permute-start(bf16[256,256]{1,0:T(8,128)(2,1)S(1)} %choose.4.mine_ref), channel_id=1, source_target_pairs={{0,16},{8,24},{16,0},{24,8},{1,17},{9,25},{17,1},{25,9},{2,18},{10... | collective-permute-start | bytes 393224 | tf_op jit(solution)/shard_map/ppermute | solution.py:106
  19.1 5.0 %collective-permute-start.11 = (bf16[256,256]{1,0:T(8,128)(2,1)S(1)}, bf16[256,256]{1,0:T(8,128)(2,1)S(1)}, u32[]{:S(2)}, u32[]{:S(2)}) collective-permute-start(bf16[256,256]{1,0:T(8,128)(2,1)S(1)} %choose.6.mine_ref), channel_id=1, source_target_pairs={{0,8},{8,0},{16,24},{24,16},{1,9},{9,1},{17,25},{25,17},{2,10},{10... | collective-permute-start | bytes 393224 | tf_op jit(solution)/shard_map/ppermute | solution.py:106
  22.3 1.9 %collective-permute-start.9 = (bf16[256,256]{1,0:T(8,128)(2,1)S(1)}, bf16[256,256]{1,0:T(8,128)(2,1)S(1)}, u32[]{:S(2)}, u32[]{:S(2)}) collective-permute-start(bf16[256,256]{1,0:T(8,128)(2,1)S(1)} %choose.5.own_k), channel_id=1, source_target_pairs={{0,1},{1,0},{2,3},{3,2},{4,5},{5,4},{6,7},{7,6},{8,9},{9,8},{10,11... | collective-permute-start | bytes 393224 | tf_op jit(solution)/shard_map/ppermute | solution.py:29
  24.1 1.4 %collective-permute-start.12 = (bf16[256,256]{1,0:T(8,128)(2,1)S(1)}, bf16[256,256]{1,0:T(8,128)(2,1)S(1)}, u32[]{:S(2)}, u32[]{:S(2)}) collective-permute-start(bf16[256,256]{1,0:T(8,128)(2,1)S(1)} %choose.7.refs_7_), channel_id=1, source_target_pairs={{0,1},{1,0},{2,3},{3,2},{4,5},{5,4},{6,7},{7,6},{8,9},{9,8},{10,11... | collective-permute-start | bytes 393224 | tf_op jit(solution)/shard_map/ppermute | solution.py:29
  25.9 5.8 %collective-permute-start.13 = (bf16[64,256]{1,0:T(8,128)(2,1)S(1)}, bf16[64,256]{1,0:T(8,128)(2,1)S(1)}, u32[]{:S(2)}, u32[]{:S(2)}) collective-permute-start(bf16[64,256]{1,0:T(8,128)(2,1)S(1)} %get-tuple-element.45), channel_id=1, source_target_pairs={{0,6},{1,7},{2,4},{3,5},{4,2},{5,3},{6,0},{7,1},{8,14},{9,15},{10,... | collective-permute-start | bytes 98312 | tf_op jit(solution)/shard_map/ppermute | solution.py:29
  29.1 4.8 %collective-permute-start.14 = (bf16[64,256]{1,0:T(8,128)(2,1)S(1)}, bf16[64,256]{1,0:T(8,128)(2,1)S(1)}, u32[]{:S(2)}, u32[]{:S(2)}) collective-permute-start(bf16[64,256]{1,0:T(8,128)(2,1)S(1)} %get-tuple-element.46), channel_id=1, source_target_pairs={{0,4},{1,5},{2,6},{3,7},{4,0},{5,1},{6,2},{7,3},{8,12},{9,13},{10,... | collective-permute-start | bytes 98312 | tf_op jit(solution)/shard_map/ppermute | solution.py:29
  29.7 4.3 %collective-permute-start.15 = (bf16[64,256]{1,0:T(8,128)(2,1)S(1)}, bf16[64,256]{1,0:T(8,128)(2,1)S(1)}, u32[]{:S(2)}, u32[]{:S(2)}) collective-permute-start(bf16[64,256]{1,0:T(8,128)(2,1)S(1)} %get-tuple-element.47), channel_id=1, source_target_pairs={{0,2},{1,3},{2,0},{3,1},{4,6},{5,7},{6,4},{7,5},{8,10},{9,11},{10,... | collective-permute-start | bytes 98312 | tf_op jit(solution)/shard_map/ppermute | solution.py:29
